TPU v7x, 32 devices: a whole 2x2x4 slice. The times are simulated.
32 devices in a mesh: cls: 8 (over z, core), ptl: 4 (over y, x).
Axes of the slice: x: 2, y: 2, z: 4, core: 2. Of those that a mesh axis runs over, the one named last changes fastest.
Arguments:
- images: bfloat16 [512, 256, 256], P(('cls', 'ptl')), may hold values from -6 to 6
- class_block: int32 [512, 1], P(('cls', 'ptl')), may hold values from 0 to 7; in each aligned block of 16 rows (0 to 15, 16 to 31, ...) at most 4 rows name the same one
- class_within: int32 [512], P(('cls', 'ptl')), may hold values from 0 to 24
- rotation: int32 [512], P(('cls', 'ptl')), may hold values from 0 to 3
- shift: int32 [512, 2], P(('cls', 'ptl')), may hold values from -8 to 8
- group: int32 [512], P(('cls', 'ptl')), may hold values from 0 to 63
- defocus: float32 [64], replicated, may hold values from 100 to 1000
Outputs:
- class_average: float32 [200, 2, 256, 256], P('cls', None, 'ptl')
Inputs may be any that keep to these rules, and one draw needn't show every extreme that they name: `class_block`: among the particles of one device at most 4 share a class block, and in every draw some device has exactly 4 in some block.
All inputs are finite; a program needn't handle non-finite values.
Results may differ from a plain program's by a relative error of at most 0.015.
Values may be sent and summed in bfloat16 or wider, within the bound.
A program may use at most 128 MiB of HBM per device.

v0:
```python
import functools
import math

import jax
import jax.numpy as jnp
import ml_dtypes
import numpy as np
from jax import lax
from jax.experimental import pallas as pl
from jax.experimental.pallas import tpu as pltpu
from jax.sharding import PartitionSpec as P

CLS_DEV = 25
SHIFT = 8
PHASE_CONTRAST = math.sqrt(0.99)
AMPLITUDE_CONTRAST = 0.1
WIENER_TERM = 1.0
OFFSET_TURNS = math.atan2(AMPLITUDE_CONTRAST, PHASE_CONTRAST) / (2.0 * math.pi)
VMEM = 48 * 1024 * 1024


def sine_coefficients():
    t = np.cos(np.linspace(0.0, math.pi / 2, 2001)[:-1]) / 2
    basis = np.stack([t ** (2 * i + 1) for i in range(8)], axis=1)
    return [float(c) for c in np.linalg.lstsq(basis, np.sin(2 * np.pi * t), rcond=None)[0]]


SINE = sine_coefficients()


def sine_of_turns(turns):
    t = turns - jnp.round(turns)
    square = t * t
    value = jnp.full_like(t, SINE[-1])
    for coefficient in SINE[-2::-1]:
        value = value * square + coefficient
    return value * t


def packed(extent):
    half = extent // 2
    index = np.arange(extent)
    is_sine = index > half
    return np.where(is_sine, index - half, index), is_sine


def tables(extent):
    frequency, is_sine = packed(extent)
    moves = np.arange(-SHIFT, SHIFT + 2)
    angle = frequency[None, :, None] * (np.arange(extent)[None, None, :] + moves[:, None, None])
    angle = (angle % extent) * (2.0 * math.pi / extent)
    value = np.where(is_sine[None, :, None], np.sin(angle), np.cos(angle)) / math.sqrt(extent)
    rows = value.astype(ml_dtypes.bfloat16)
    return rows, np.ascontiguousarray(rows.transpose(0, 2, 1))


def row_expansion(extent, parts):
    half = extent // 2
    each = extent // parts
    out = np.zeros((parts, 2, each, extent), np.float32)
    for ky in range(extent):
        size = min(ky, extent - ky)
        out[ky // each, 0, ky % each, size] = 1.0
        if 0 < size < half:
            out[ky // each, 1, ky % each, half + size] = 1.0 if ky < half else -1.0
    return out.reshape(2 * extent, extent).astype(ml_dtypes.bfloat16)


def column_expansion(extent):
    half = extent // 2
    out = np.zeros((extent, 2, extent), np.float32)
    for kx in range(extent):
        size = min(kx, extent - kx)
        out[size, 0, kx] = 1.0
        if 0 < size < half:
            out[half + size, 1, kx] = -1.0 if kx < half else 1.0
    return out.reshape(extent, 2 * extent).astype(ml_dtypes.bfloat16)


def transform_kernel(slot, info, defocus, image, rows, columns, radius, out, turned):
    particle = pl.program_id(0)
    extent = image.shape[-1]
    turn = info[particle, 0]
    shift_x = info[particle, 1]
    shift_y = info[particle, 2]
    flip_x = turn >= 2
    flip_y = (turn == 1) | (turn == 2)
    move_x = jnp.where(flip_x, 1 - shift_x, shift_x) + SHIFT
    move_y = jnp.where(flip_y, 1 - shift_y, shift_y) + SHIFT
    odd = turn % 2 == 1

    @pl.when(odd)
    def _():
        turned[...] = image[0].T

    @pl.when(jnp.logical_not(odd))
    def _():
        turned[...] = image[0]

    along_x = jnp.dot(turned[...], columns[move_x], preferred_element_type=jnp.float32)
    spectrum = jnp.dot(
        rows[move_y], along_x.astype(jnp.bfloat16), preferred_element_type=jnp.float32
    )
    scale = defocus[info[particle, 3]] * (1.0 / (2.0 * math.pi))
    contrast = -sine_of_turns(radius[...] * scale + OFFSET_TURNS)
    half = extent // 2
    row_sine = lax.broadcasted_iota(jnp.int32, (extent, 1), 0) > half
    column_sine = lax.broadcasted_iota(jnp.int32, (1, extent), 1) > half
    sign_y = jnp.where(flip_y, -1.0, 1.0)
    sign_x = jnp.where(flip_x, -1.0, 1.0)
    signs = jnp.where(row_sine, sign_y, 1.0) * jnp.where(column_sine, sign_x, 1.0)
    out[0] = (spectrum * (contrast * signs)).astype(jnp.bfloat16)


def class_kernel(sources, capacity, number, per_step, labels, block, slots, expand, out, total):
    step = pl.program_id(0)
    loads = sources

    @pl.when(step == 0)
    def _():
        total[...] = jnp.zeros_like(total)

    @pl.when(step < loads)
    def _():
        def body(particle, filled):
            label = labels[step * number + particle]
            mine = label // CLS_DEV == block[0]

            @pl.when(mine)
            def _():
                within = label % CLS_DEV
                total[within] += slots[filled].astype(jnp.float32)

            return filled + mine.astype(jnp.int32)

        lax.fori_loop(0, number, body, jnp.int32(0))

    @pl.when(step >= loads)
    def _():
        parts, _, double, extent = out.shape
        for item in range(per_step):
            value = total[(step - loads) * per_step + item].astype(jnp.bfloat16)
            laid = jnp.dot(expand[...], value, preferred_element_type=jnp.float32)
            laid = laid.astype(jnp.bfloat16)
            for part in range(parts):
                out[part, item] = laid[part * double : (part + 1) * double]


def weight_kernel(labels, groups, block, defocus, radius, out):
    out[...] = jnp.zeros_like(out)

    def body(particle, carry):
        label = labels[particle]

        @pl.when(label // CLS_DEV == block[0])
        def _():
            scale = defocus[groups[particle]] * (1.0 / (2.0 * math.pi))
            contrast = sine_of_turns(radius[...] * scale + OFFSET_TURNS)
            within = label % CLS_DEV
            out[within] += contrast * contrast

        return carry

    lax.fori_loop(0, labels.shape[0], body, 0)


def final_kernel(per_step, received, weight, expand, out):
    parts = received.shape[0]
    _, _, each, extent = out.shape
    for item in range(per_step):
        value = received[0, item].astype(jnp.float32)
        for part in range(1, parts):
            value = value + received[part, item].astype(jnp.float32)
        wide = jnp.dot(value.astype(jnp.bfloat16), expand[...], preferred_element_type=jnp.float32)
        inverse = 1.0 / (weight[item] + WIENER_TERM)
        out[item, 0] = (wide[:each, :extent] + wide[each:, extent:]) * inverse
        out[item, 1] = (wide[:each, extent:] - wide[each:, :extent]) * inverse


def params():
    return pltpu.CompilerParams(vmem_limit_bytes=VMEM)


def per_device(images, class_block, class_within, rotation, shift, group, defocus):
    blocks = lax.axis_size("cls")
    parts = lax.axis_size("ptl")
    number, extent, _ = images.shape
    each = extent // parts
    capacity = 2 * number // blocks
    me = lax.axis_index("cls").astype(jnp.int32)
    part = lax.axis_index("ptl").astype(jnp.int32)
    target = class_block[:, 0]
    same = target[:, None] == target[None, :]
    before = jnp.arange(number)[:, None] > jnp.arange(number)[None, :]
    slot = target * capacity + jnp.sum((same & before).astype(jnp.int32), axis=1)
    info = jnp.stack([rotation, shift[:, 0], shift[:, 1], group], axis=1)

    klass = target * CLS_DEV + class_within
    own = jnp.stack([klass, group], axis=0)
    labels = lax.all_gather(own, ("cls", "ptl"), axis=0)
    labels = labels.reshape(blocks, parts, 2, number)
    all_class = labels[:, :, 0].reshape(-1)
    all_group = labels[:, :, 1].reshape(-1)
    column_class = lax.dynamic_index_in_dim(labels[:, :, 0], part, 1, keepdims=False).reshape(-1)

    frequency, _ = packed(extent)
    share = (frequency / extent) ** 2
    packed_radius = (share[:, None] + share[None, :]).astype(np.float32)
    row_table, column_table = tables(extent)

    whole = lambda shape: pl.BlockSpec(shape, lambda *_: (0,) * len(shape))
    outgoing = pl.pallas_call(
        transform_kernel,
        grid_spec=pltpu.PrefetchScalarGridSpec(
            num_scalar_prefetch=3,
            grid=(number,),
            in_specs=[
                pl.BlockSpec((1, extent, extent), lambda i, *_: (i, 0, 0)),
                whole(row_table.shape),
                whole(column_table.shape),
                whole((extent, extent)),
            ],
            out_specs=pl.BlockSpec((1, extent, extent), lambda i, slot, *_: (slot[i], 0, 0)),
            scratch_shapes=[pltpu.VMEM((extent, extent), jnp.bfloat16)],
        ),
        out_shape=jax.ShapeDtypeStruct((blocks * capacity, extent, extent), jnp.bfloat16),
        compiler_params=params(),
        name="transform",
    )(slot, info, defocus, images, row_table, column_table, packed_radius)
    arrived = lax.all_to_all(
        outgoing.reshape(blocks, capacity, extent, extent), "cls", 0, 0, tiled=True
    ).reshape(blocks * capacity, extent, extent)

    ky = part * each + jnp.arange(each, dtype=jnp.int32)
    kx = np.minimum(np.arange(extent), extent - np.arange(extent))
    ky = jnp.minimum(ky, extent - ky).astype(jnp.float32) / extent
    radius = ky[:, None] * ky[:, None] + ((kx / extent) ** 2).astype(np.float32)[None, :]
    smem = pl.BlockSpec(memory_space=pltpu.SMEM)
    vmem = pl.BlockSpec(memory_space=pltpu.VMEM)
    weight = pl.pallas_call(
        weight_kernel,
        in_specs=[smem, smem, smem, smem, vmem],
        out_specs=vmem,
        out_shape=jax.ShapeDtypeStruct((CLS_DEV, each, extent), jnp.float32),
        compiler_params=params(),
        cost_estimate=pl.CostEstimate(
            flops=40 * number * parts * each * extent, bytes_accessed=2**21, transcendentals=0
        ),
        name="weights",
    )(all_class, all_group, me[None], defocus, radius)

    per_step = 5
    steps = CLS_DEV // per_step
    partial = pl.pallas_call(
        functools.partial(class_kernel, blocks, capacity, number, per_step),
        grid_spec=pltpu.PrefetchScalarGridSpec(
            num_scalar_prefetch=2,
            grid=(blocks + steps,),
            in_specs=[
                pl.BlockSpec(
                    (capacity, extent, extent), lambda i, *_: (jnp.minimum(i, blocks - 1), 0, 0)
                ),
                whole((2 * extent, extent)),
            ],
            out_specs=pl.BlockSpec(
                (parts, per_step, 2 * each, extent),
                lambda i, *_: (0, jnp.maximum(i - blocks, 0), 0, 0),
            ),
            scratch_shapes=[pltpu.VMEM((CLS_DEV, extent, extent), jnp.float32)],
        ),
        out_shape=jax.ShapeDtypeStruct((parts, CLS_DEV, 2 * each, extent), jnp.bfloat16),
        compiler_params=params(),
        name="classes",
    )(column_class, me[None], arrived, row_expansion(extent, parts))
    received = lax.all_to_all(partial, "ptl", 0, 0, tiled=True)

    return pl.pallas_call(
        functools.partial(final_kernel, per_step),
        grid=(steps,),
        in_specs=[
            pl.BlockSpec((parts, per_step, 2 * each, extent), lambda i: (0, i, 0, 0)),
            pl.BlockSpec((per_step, each, extent), lambda i: (i, 0, 0)),
            whole((extent, 2 * extent)),
        ],
        out_specs=pl.BlockSpec((per_step, 2, each, extent), lambda i: (i, 0, 0, 0)),
        out_shape=jax.ShapeDtypeStruct((CLS_DEV, 2, each, extent), jnp.float32),
        compiler_params=params(),
        name="finish",
    )(received, weight, column_expansion(extent))


def solution(mesh):
    return jax.shard_map(
        per_device,
        mesh=mesh,
        in_specs=(
            P(("cls", "ptl"), None, None),
            P(("cls", "ptl"), None),
            P(("cls", "ptl")),
            P(("cls", "ptl")),
            P(("cls", "ptl"), None),
            P(("cls", "ptl")),
            P(),
        ),
        out_specs=P("cls", None, "ptl", None),
        check_vma=False,
    )
```

profile of v0, /device:TPU:0, one launch (start us, length us, event | category | flops | bytes accessed | tf_op | source)
XLA Modules:
  0.0 255.1 jit_solution(4510416936965936429)
XLA Ops:
  0.0 0.9 convert_reduce_fusion
  0.9 0.7 pad_add_fusion
  1.6 0.1 copy.25.info
  1.7 0.7 multiply_add_fusion
  2.4 1.7 copy-done
  4.0 1.6 copy-done.1
  5.6 0.9 copy-done.4
  6.6 0.7 copy-done.5
  7.2 12.0 %transform.1 = bf16[32,256,256]{2,1,0:T(8,128)(2,1)} custom-call(s32[16]{0:T(128)S(1)} %get-tuple-element.7.slot, s32[16,4]{1,0:T(8,128)S(1)} %copy.25.info, f32[64]{0:T(128)S(1)} %copy-done.5, bf16[16,256,256]{2,1,0:T(8,128)(2,1)S(1)} %copy-done.1, bf16[18,256,256]{2,1,0:T(8,128)(2,1)S(1)} %copy-done, bf16[18,256,256]{2,1,0:T(8,128)(2,1)} %constant.40.clone.columns, ...), custom_call_target="tpu_custom_call" | custom-call | tf_op jit(solution)/shard_map/transform/pallas_call | solution.py:212
  19.3 6.6 %all-to-all-start = ((bf16[8,4,256,256]{3,2,1,0:T(8,128)(2,1)}), bf16[8,4,256,256]{3,2,1,0:T(8,128)(2,1)}, u32[]{:S(2)}, u32[]{:S(2)}) async-start(bf16[8,4,256,256]{3,2,1,0:T(8,128)(2,1)} %bitcast.17), calls=%async_computation | async-start | bytes 8388608 | tf_op jit(solution)/shard_map/all_to_all | solution.py:230
  25.9 0.0 copy-done.7
  25.9 130.2 %all-gather.1 = s32[32,2,16]{2,1,0:T(2,128)S(1)} all-gather(s32[1,2,16]{2,1,0:T(2,128)S(1)} %add_bitcast_fusion), channel_id=2, replica_groups=mesh['cls'=8,'ptl'=4] {'cls','ptl'}, dimensions={0}, use_global_device_ids=true | all-gather | bytes 4224 | tf_op jit(solution)/shard_map/all_gather | solution.py:200
  156.1 0.1 slice_reduce_fusion
  156.2 0.1 reshape.27.labels
  156.2 0.0 all-to-all-done
  156.3 0.0 copy-done.3
  156.3 12.5 %classes.1 = bf16[4,25,128,256]{3,2,1,0:T(8,128)(2,1)} custom-call(s32[128]{0:T(128)S(1)} %reshape.27.labels, s32[1]{0:T(128)} %bitcast.5.block, bf16[32,256,256]{2,1,0:T(8,128)(2,1)} %bitcast.9.slots, bf16[512,256]{1,0:T(8,128)(2,1)S(1)} %copy-done.3), custom_call_target="tpu_custom_call" | custom-call | tf_op jit(solution)/shard_map/classes/pallas_call | solution.py:254
  168.7 5.4 %all-to-all-start.1 = ((bf16[4,25,128,256]{3,2,1,0:T(8,128)(2,1)}), bf16[4,25,128,256]{3,2,1,0:T(8,128)(2,1)}, u32[]{:S(2)}, u32[]{:S(2)}) async-start(bf16[4,25,128,256]{3,2,1,0:T(8,128)(2,1)} %classes.1), calls=%async_computation.1 | async-start | bytes 13107200 | tf_op jit(solution)/shard_map/all_to_all | solution.py:275
  174.2 0.1 reshape_squeeze.6.labels
  174.3 0.1 reshape_squeeze.7.groups
  174.4 0.1 broadcast_add_fusion.radius
  174.5 20.3 %weights.1.weight = f32[25,64,256]{2,1,0:T(8,128)S(1)} custom-call(s32[512]{0:T(512)S(1)} %reshape_squeeze.6.labels, s32[512]{0:T(512)S(1)} %reshape_squeeze.7.groups, s32[1]{0:T(128)} %bitcast.5.block, f32[64]{0:T(128)S(1)} %copy-done.6, f32[64,256]{1,0:T(8,128)S(1)} %broadcast_add_fusion.radius), custom_call_target="tpu_custom_call" | custom-call | flops 41943040 | bytes 2097152 | tf_op jit(solution)/shard_map/weights/pallas_call | solution.py:240
  194.8 53.4 %all-to-all-done.1.received = bf16[4,25,128,256]{3,2,1,0:T(8,128)(2,1)} async-done(((bf16[4,25,128,256]{3,2,1,0:T(8,128)(2,1)}), bf16[4,25,128,256]{3,2,1,0:T(8,128)(2,1)}, u32[]{:S(2)}, u32[]{:S(2)}) %all-to-all-start.1) | async-done | bytes 6553632 | tf_op jit(solution)/shard_map/all_to_all | solution.py:275
  248.2 6.9 %finish.1 = f32[25,2,64,256]{3,2,1,0:T(8,128)} custom-call(bf16[4,25,128,256]{3,2,1,0:T(8,128)(2,1)} %all-to-all-done.1.received, f32[25,64,256]{2,1,0:T(8,128)S(1)} %weights.1.weight, bf16[256,512]{1,0:T(8,128)(2,1)S(1)} %copy-done.2), custom_call_target="tpu_custom_call" | custom-call | tf_op jit(solution)/shard_map/finish/pallas_call | solution.py:277
  (15 shorter events, 0.1 us)
Async XLA Ops:
  2.4 1.7 copy-start
  4.0 1.6 copy-start.1
  5.6 0.9 copy-start.4
  6.6 0.7 copy-start.5
  19.3 6.6 %copy-start.7 = (s32[16]{0:T(128)S(1)}, s32[16]{0:T(128)}, u32[]{:S(2)}) copy-start(s32[16]{0:T(128)} %param.18) | copy-start | bytes 196
  19.3 137.0 %copy-start.3 = (bf16[512,256]{1,0:T(8,128)(2,1)S(1)}, bf16[512,256]{1,0:T(8,128)(2,1)}, u32[]{:S(2)}) copy-start(bf16[512,256]{1,0:T(8,128)(2,1)} %constant.43.clone.expand) | copy-start | bytes 786436
  19.3 137.0 %all-to-all-start = ((bf16[8,4,256,256]{3,2,1,0:T(8,128)(2,1)}), bf16[8,4,256,256]{3,2,1,0:T(8,128)(2,1)}, u32[]{:S(2)}, u32[]{:S(2)}) async-start(bf16[8,4,256,256]{3,2,1,0:T(8,128)(2,1)} %bitcast.17), calls=%async_computation | async-start | bytes 8388608 | tf_op jit(solution)/shard_map/all_to_all | solution.py:230
  168.7 5.6 %copy-start.8 = (f32[256]{0:T(256)S(1)}, f32[256]{0:T(256)}, u32[]{:S(2)}) copy-start(f32[256]{0:T(256)} %constant.51) | copy-start | bytes 3076
  168.7 5.7 %copy-start.6 = (f32[64]{0:T(128)S(1)}, f32[64]{0:T(128)}, u32[]{:S(2)}) copy-start(f32[64]{0:T(128)} %defocus.3) | copy-start | bytes 772
  168.7 79.5 %copy-start.2 = (bf16[256,512]{1,0:T(8,128)(2,1)S(1)}, bf16[256,512]{1,0:T(8,128)(2,1)}, u32[]{:S(2)}) copy-start(bf16[256,512]{1,0:T(8,128)(2,1)} %constant.44.clone.expand) | copy-start | bytes 786436
  168.7 79.5 %all-to-all-start.1 = ((bf16[4,25,128,256]{3,2,1,0:T(8,128)(2,1)}), bf16[4,25,128,256]{3,2,1,0:T(8,128)(2,1)}, u32[]{:S(2)}, u32[]{:S(2)}) async-start(bf16[4,25,128,256]{3,2,1,0:T(8,128)(2,1)} %classes.1), calls=%async_computation.1 | async-start | bytes 13107200 | tf_op jit(solution)/shard_map/all_to_all | solution.py:275
where the time goes:
time: 260 us; the launch traced here: 255 us
  blocking collectives  130 us (50%)
  waiting for transfers between devices  53.4 us (21%)
  Pallas kernels  51.7 us (20%)
  starting transfers between devices  12 us (5%)
  local copies, waits for them, and re-layouts  5.3 us (2%)
    all_gather x1, blocking collectives, per_device(): labels = lax.all_gather(own, ('cls', 'ptl'), axis=0)  130 us
    all_to_all x1, waiting for transfers between devices, per_device(): received = lax.all_to_all(partial, 'ptl', 0, 0, tiled=True)  53.4 us
    pallas_call x1, Pallas kernels, per_device(): pl.pallas_call(weight_kernel, in_specs=[smem, smem, smem, smem, vmem], ou...  20.3 us
    pallas_call x1, Pallas kernels, per_device(): pl.pallas_call(functools.partial(class_kernel, blocks, capacity, number,...  12.5 us
    pallas_call x1, Pallas kernels, per_device(): pl.pallas_call(transform_kernel, grid_spec=pltpu.PrefetchScalarGridSpec(n...  12 us
    pallas_call x1, Pallas kernels, per_device(): pl.pallas_call(functools.partial(final_kernel, per_step), grid=(steps,),...  6.89 us
    all_to_all x1, starting transfers between devices, per_device(): lax.all_to_all(outgoing.reshape(blocks, capacity, extent, extent), 'cls',...  6.58 us
    all_to_all x1, starting transfers between devices, per_device(): received = lax.all_to_all(partial, 'ptl', 0, 0, tiled=True)  5.43 us
  transfers between devices with their start and end apart: 2, of which 1 were waited for; matrix products, arithmetic and copies ran while one was open for 0% of the time, Pallas kernels for 8%

commit v1 on v0

--- a/solution.py
+++ b/solution.py
@@ -21,7 +21,7 @@
 
 def sine_coefficients():
     t = np.cos(np.linspace(0.0, math.pi / 2, 2001)[:-1]) / 2
-    basis = np.stack([t ** (2 * i + 1) for i in range(8)], axis=1)
+    basis = np.stack([t ** (2 * i + 1) for i in range(7)], axis=1)
     return [float(c) for c in np.linalg.lstsq(basis, np.sin(2 * np.pi * t), rcond=None)[0]]
 
 
@@ -198,6 +198,7 @@
     klass = target * CLS_DEV + class_within
     own = jnp.stack([klass, group], axis=0)
     labels = lax.all_gather(own, ("cls", "ptl"), axis=0)
+    images, labels = lax.optimization_barrier((images, labels))
     labels = labels.reshape(blocks, parts, 2, number)
     all_class = labels[:, :, 0].reshape(-1)
     all_group = labels[:, :, 1].reshape(-1)

time: 260 us -> 286 us (1.10); the launches traced: 255 us -> 286 us
  waiting for transfers between devices: 53.4 us -> 152 us
  blocking collectives: 130 us -> 69.7 us
  Pallas kernels: 51.7 us -> 45.4 us
    all_to_all x1, waiting for transfers between devices: 0.01 us -> 93.8 us  [per_device(): lax.all_to_all(outgoing.reshape(blocks, capacity, extent, extent), 'cls',...]
    all_gather x1, blocking collectives: 130 us -> 69.7 us  [per_device(): labels = lax.all_gather(own, ('cls', 'ptl'), axis=0)]
    pallas_call x1, Pallas kernels: 20.3 us -> 14.8 us  [per_device(): pl.pallas_call(weight_kernel, in_specs=[smem, smem, smem, smem, vmem], ou...]
    all_to_all x1, waiting for transfers between devices: 53.4 us -> 58.4 us  [per_device(): received = lax.all_to_all(partial, 'ptl', 0, 0, tiled=True)]
  transfers between devices with their start and end apart: 2 -> 2, of which waited for: 1 -> 2; matrix products, arithmetic and copies ran while one was open for 0% -> 0% of each run, Pallas kernels for 8% -> 5%
where the time goes in v1:
time: 286 us
  waiting for transfers between devices  152 us (53%)
  blocking collectives  69.7 us (24%)
  Pallas kernels  45.4 us (16%)
  starting transfers between devices  10.1 us (4%)
  local copies, waits for them, and re-layouts  5.3 us (2%)
  other arithmetic  3.03 us (1%)
    all_to_all x1, waiting for transfers between devices, per_device(): lax.all_to_all(outgoing.reshape(blocks, capacity, extent, extent), 'cls',...  93.8 us
    all_gather x1, blocking collectives, per_device(): labels = lax.all_gather(own, ('cls', 'ptl'), axis=0)  69.7 us
    all_to_all x1, waiting for transfers between devices, per_device(): received = lax.all_to_all(partial, 'ptl', 0, 0, tiled=True)  58.4 us
    pallas_call x1, Pallas kernels, per_device(): pl.pallas_call(weight_kernel, in_specs=[smem, smem, smem, smem, vmem], ou...  14.8 us
    pallas_call x1, Pallas kernels, per_device(): pl.pallas_call(transform_kernel, grid_spec=pltpu.PrefetchScalarGridSpec(n...  12 us
    pallas_call x1, Pallas kernels, per_device(): pl.pallas_call(functools.partial(class_kernel, blocks, capacity, number,...  11.7 us
    pallas_call x1, Pallas kernels, per_device(): pl.pallas_call(functools.partial(final_kernel, per_step), grid=(steps,),...  6.89 us
  transfers between devices with their start and end apart: 2, of which 2 were waited for; matrix products, arithmetic and copies ran while one was open for 0% of the time, Pallas kernels for 5%

profile of v1, /device:TPU:0, one launch (start us, length us, event | category | flops | bytes accessed | tf_op | source)
XLA Modules:
  0.0 285.9 jit_solution(16217305652778751046)
XLA Ops:
  0.0 0.9 convert_reduce_fusion
  0.9 0.7 multiply_add_fusion
  1.6 0.7 add_bitcast_fusion
  2.3 69.7 %all-gather.1 = s32[32,2,16]{2,1,0:T(2,128)S(1)} all-gather(s32[1,2,16]{2,1,0:T(2,128)S(1)} %add_bitcast_fusion), channel_id=2, replica_groups=mesh['cls'=8,'ptl'=4] {'cls','ptl'}, dimensions={0}, use_global_device_ids=true | all-gather | bytes 4224 | tf_op jit(solution)/shard_map/all_gather | solution.py:200
  72.0 0.7 pad_add_fusion
  72.7 0.1 copy.25.info
  72.8 1.7 copy-done
  74.4 1.6 copy-done.1
  76.0 0.9 copy-done.4
  77.0 0.7 copy-done.5
  77.6 12.0 %transform.1 = bf16[32,256,256]{2,1,0:T(8,128)(2,1)} custom-call(s32[16]{0:T(128)S(1)} %get-tuple-element.11.slot, s32[16,4]{1,0:T(8,128)S(1)} %copy.25.info, f32[64]{0:T(128)S(1)} %copy-done.5, bf16[16,256,256]{2,1,0:T(8,128)(2,1)S(1)} %copy-done.1, bf16[18,256,256]{2,1,0:T(8,128)(2,1)S(1)} %copy-done, bf16[18,256,256]{2,1,0:T(8,128)(2,1)} %constant.40.clone.columns, ...), custom_call_target="tpu_custom_call" | custom-call | tf_op jit(solution)/shard_map/transform/pallas_call | solution.py:213
  89.6 4.7 %all-to-all-start = ((bf16[8,4,256,256]{3,2,1,0:T(8,128)(2,1)}), bf16[8,4,256,256]{3,2,1,0:T(8,128)(2,1)}, u32[]{:S(2)}, u32[]{:S(2)}) async-start(bf16[8,4,256,256]{3,2,1,0:T(8,128)(2,1)} %bitcast.17), calls=%async_computation | async-start | bytes 8388608 | tf_op jit(solution)/shard_map/all_to_all | solution.py:231
  94.3 0.1 slice_reduce_fusion
  94.4 0.1 reshape.27.labels
  94.5 93.8 %all-to-all-done = bf16[8,4,256,256]{3,2,1,0:T(8,128)(2,1)} async-done(((bf16[8,4,256,256]{3,2,1,0:T(8,128)(2,1)}), bf16[8,4,256,256]{3,2,1,0:T(8,128)(2,1)}, u32[]{:S(2)}, u32[]{:S(2)}) %all-to-all-start) | async-done | bytes 4194336 | tf_op jit(solution)/shard_map/all_to_all | solution.py:231
  188.3 11.7 %classes.1 = bf16[4,25,128,256]{3,2,1,0:T(8,128)(2,1)} custom-call(s32[128]{0:T(128)S(1)} %reshape.27.labels, s32[1]{0:T(128)} %bitcast.5.block, bf16[32,256,256]{2,1,0:T(8,128)(2,1)} %bitcast.9.slots, bf16[512,256]{1,0:T(8,128)(2,1)S(1)} %copy-done.3), custom_call_target="tpu_custom_call" | custom-call | tf_op jit(solution)/shard_map/classes/pallas_call | solution.py:255
  200.0 5.4 %all-to-all-start.1 = ((bf16[4,25,128,256]{3,2,1,0:T(8,128)(2,1)}), bf16[4,25,128,256]{3,2,1,0:T(8,128)(2,1)}, u32[]{:S(2)}, u32[]{:S(2)}) async-start(bf16[4,25,128,256]{3,2,1,0:T(8,128)(2,1)} %classes.1), calls=%async_computation.1 | async-start | bytes 13107200 | tf_op jit(solution)/shard_map/all_to_all | solution.py:276
  205.5 0.1 reshape_squeeze.6.labels
  205.6 0.1 reshape_squeeze.7.groups
  205.7 0.1 broadcast_add_fusion.radius
  205.7 14.8 %weights.1.weight = f32[25,64,256]{2,1,0:T(8,128)S(1)} custom-call(s32[512]{0:T(512)S(1)} %reshape_squeeze.6.labels, s32[512]{0:T(512)S(1)} %reshape_squeeze.7.groups, s32[1]{0:T(128)} %bitcast.5.block, f32[64]{0:T(128)S(1)} %copy-done.6, f32[64,256]{1,0:T(8,128)S(1)} %broadcast_add_fusion.radius), custom_call_target="tpu_custom_call" | custom-call | flops 41943040 | bytes 2097152 | tf_op jit(solution)/shard_map/weights/pallas_call | solution.py:241
  220.5 58.4 %all-to-all-done.1.received = bf16[4,25,128,256]{3,2,1,0:T(8,128)(2,1)} async-done(((bf16[4,25,128,256]{3,2,1,0:T(8,128)(2,1)}), bf16[4,25,128,256]{3,2,1,0:T(8,128)(2,1)}, u32[]{:S(2)}, u32[]{:S(2)}) %all-to-all-start.1) | async-done | bytes 6553632 | tf_op jit(solution)/shard_map/all_to_all | solution.py:276
  279.0 0.0 copy-done.2
  279.0 6.9 %finish.1 = f32[25,2,64,256]{3,2,1,0:T(8,128)} custom-call(bf16[4,25,128,256]{3,2,1,0:T(8,128)(2,1)} %all-to-all-done.1.received, f32[25,64,256]{2,1,0:T(8,128)S(1)} %weights.1.weight, bf16[256,512]{1,0:T(8,128)(2,1)S(1)} %copy-done.2), custom_call_target="tpu_custom_call" | custom-call | tf_op jit(solution)/shard_map/finish/pallas_call | solution.py:278
  (13 shorter events, 0.1 us)
Async XLA Ops:
  72.8 1.7 copy-start
  74.4 1.6 copy-start.1
  76.0 0.9 copy-start.4
  77.0 0.7 copy-start.5
  89.6 98.7 %copy-start.3 = (bf16[512,256]{1,0:T(8,128)(2,1)S(1)}, bf16[512,256]{1,0:T(8,128)(2,1)}, u32[]{:S(2)}) copy-start(bf16[512,256]{1,0:T(8,128)(2,1)} %constant.43.clone.expand) | copy-start | bytes 786436
  89.6 98.7 %all-to-all-start = ((bf16[8,4,256,256]{3,2,1,0:T(8,128)(2,1)}), bf16[8,4,256,256]{3,2,1,0:T(8,128)(2,1)}, u32[]{:S(2)}, u32[]{:S(2)}) async-start(bf16[8,4,256,256]{3,2,1,0:T(8,128)(2,1)} %bitcast.17), calls=%async_computation | async-start | bytes 8388608 | tf_op jit(solution)/shard_map/all_to_all | solution.py:231
  200.0 5.6 %copy-start.7 = (f32[256]{0:T(256)S(1)}, f32[256]{0:T(256)}, u32[]{:S(2)}) copy-start(f32[256]{0:T(256)} %constant.51) | copy-start | bytes 3076
  200.0 5.7 %copy-start.6 = (f32[64]{0:T(128)S(1)}, f32[64]{0:T(128)}, u32[]{:S(2)}) copy-start(f32[64]{0:T(128)} %defocus.3) | copy-start | bytes 772
  200.0 78.9 %copy-start.2 = (bf16[256,512]{1,0:T(8,128)(2,1)S(1)}, bf16[256,512]{1,0:T(8,128)(2,1)}, u32[]{:S(2)}) copy-start(bf16[256,512]{1,0:T(8,128)(2,1)} %constant.44.clone.expand) | copy-start | bytes 786436
  200.0 78.9 %all-to-all-start.1 = ((bf16[4,25,128,256]{3,2,1,0:T(8,128)(2,1)}), bf16[4,25,128,256]{3,2,1,0:T(8,128)(2,1)}, u32[]{:S(2)}, u32[]{:S(2)}) async-start(bf16[4,25,128,256]{3,2,1,0:T(8,128)(2,1)} %classes.1), calls=%async_computation.1 | async-start | bytes 13107200 | tf_op jit(solution)/shard_map/all_to_all | solution.py:276

commit v2 on v1

--- a/solution.py
+++ b/solution.py
@@ -197,12 +197,15 @@
 
     klass = target * CLS_DEV + class_within
     own = jnp.stack([klass, group], axis=0)
-    labels = lax.all_gather(own, ("cls", "ptl"), axis=0)
-    images, labels = lax.optimization_barrier((images, labels))
-    labels = labels.reshape(blocks, parts, 2, number)
+    column = lax.all_to_all(
+        jnp.broadcast_to(own[None], (blocks, 2, number)), "cls", 0, 0, tiled=True
+    )
+    labels = lax.all_to_all(
+        jnp.broadcast_to(column[None], (parts, blocks, 2, number)), "ptl", 0, 0, tiled=True
+    )
     all_class = labels[:, :, 0].reshape(-1)
     all_group = labels[:, :, 1].reshape(-1)
-    column_class = lax.dynamic_index_in_dim(labels[:, :, 0], part, 1, keepdims=False).reshape(-1)
+    column_class = column[:, 0].reshape(-1)
 
     frequency, _ = packed(extent)
     share = (frequency / extent) ** 2

time: 286 us -> 228 us (0.80)
  blocking collectives: 69.7 us -> 0 us
  starting transfers between devices: 10.1 us -> 20.6 us
  waiting for transfers between devices: 152 us -> 148 us
    all_gather x1 -> x0, blocking collectives: 69.7 us -> none  [per_device(): labels = lax.all_gather(own, ('cls', 'ptl'), axis=0)]
    all_to_all x0 -> x2, starting transfers between devices: none -> 9.94 us  [the longest x1 6.33 us: per_device(): lax.all_to_all(jnp.broadcast_to(own[None], (blocks, 2, number)), 'cls', 0...]
    all_to_all x1, waiting for transfers between devices: 58.4 us -> 54.5 us  [per_device(): received = lax.all_to_all(partial, 'ptl', 0, 0, tiled=True)]
  transfers between devices with their start and end apart: 2 -> 4, of which waited for: 2 -> 2; matrix products, arithmetic and copies ran while one was open for 0% -> 1% of each run, Pallas kernels for 5% -> 18%
where the time goes in v2:
time: 228 us; the launch traced here: 227 us
  waiting for transfers between devices  148 us (65%)
  Pallas kernels  47.7 us (21%)
  starting transfers between devices  20.6 us (9%)
  local copies, waits for them, and re-layouts  7.24 us (3%)
  other arithmetic  3.7 us (2%)
    all_to_all x1, waiting for transfers between devices, per_device(): lax.all_to_all(outgoing.reshape(blocks, capacity, extent, extent), 'cls',...  93.4 us
    all_to_all x1, waiting for transfers between devices, per_device(): received = lax.all_to_all(partial, 'ptl', 0, 0, tiled=True)  54.5 us
    pallas_call x1, Pallas kernels, per_device(): pl.pallas_call(weight_kernel, in_specs=[smem, smem, smem, smem, vmem], ou...  16.4 us
    pallas_call x1, Pallas kernels, per_device(): pl.pallas_call(functools.partial(class_kernel, blocks, capacity, number,...  12.3 us
    pallas_call x1, Pallas kernels, per_device(): pl.pallas_call(transform_kernel, grid_spec=pltpu.PrefetchScalarGridSpec(n...  12.1 us
    pallas_call x1, Pallas kernels, per_device(): pl.pallas_call(functools.partial(final_kernel, per_step), grid=(steps,),...  6.88 us
    all_to_all x1, starting transfers between devices, per_device(): lax.all_to_all(jnp.broadcast_to(own[None], (blocks, 2, number)), 'cls', 0...  6.33 us
    unnamed x18, local copies, waits for them, and re-layouts  5.68 us
  transfers between devices with their start and end apart: 4, of which 2 were waited for; matrix products, arithmetic and copies ran while one was open for 1% of the time, Pallas kernels for 18%

profile of v2, /device:TPU:0, one launch (start us, length us, event | category | flops | bytes accessed | tf_op | source)
XLA Modules:
  0.0 227.2 jit_solution(11851474921077226986)
XLA Ops:
  0.0 0.9 convert_reduce_fusion
  0.9 0.7 multiply_add_fusion
  1.6 0.7 pad_add_fusion.1
  2.3 0.6 broadcast_in_dim.6
  2.9 6.3 %all-to-all-start = ((s32[8,2,16]{2,1,0:T(2,128)}), s32[8,2,16]{2,1,0:T(2,128)S(1)}, u32[]{:S(2)}, u32[]{:S(2)}) async-start(s32[8,2,16]{2,1,0:T(2,128)} %broadcast_in_dim.6), calls=%async_computation | async-start | bytes 16384 | tf_op jit(solution)/shard_map/all_to_all | solution.py:200
  9.2 0.7 pad_add_fusion
  10.0 1.7 copy-done
  11.6 1.6 copy-done.1
  13.2 0.9 copy-done.4
  14.2 0.7 copy-done.5
  14.8 12.1 %transform.1 = bf16[32,256,256]{2,1,0:T(8,128)(2,1)} custom-call(s32[16]{0:T(128)S(1)} %get-tuple-element.7.slot, s32[16,4]{1,0:T(8,128)S(1)} %copy.19.info, f32[64]{0:T(128)S(1)} %copy-done.5, bf16[16,256,256]{2,1,0:T(8,128)(2,1)S(1)} %copy-done.1, bf16[18,256,256]{2,1,0:T(8,128)(2,1)S(1)} %copy-done, bf16[18,256,256]{2,1,0:T(8,128)(2,1)} %constant.35.clone.columns, ...), custom_call_target="tpu_custom_call" | custom-call | tf_op jit(solution)/shard_map/transform/pallas_call | solution.py:216
  26.9 5.2 %all-to-all-start.1 = ((bf16[8,4,256,256]{3,2,1,0:T(8,128)(2,1)}), bf16[8,4,256,256]{3,2,1,0:T(8,128)(2,1)}, u32[]{:S(2)}, u32[]{:S(2)}) async-start(bf16[8,4,256,256]{3,2,1,0:T(8,128)(2,1)} %bitcast.11), calls=%async_computation.1 | async-start | bytes 8388608 | tf_op jit(solution)/shard_map/all_to_all | solution.py:234
  32.2 0.7 reshape.38
  32.9 93.4 %all-to-all-done.1 = bf16[8,4,256,256]{3,2,1,0:T(8,128)(2,1)} async-done(((bf16[8,4,256,256]{3,2,1,0:T(8,128)(2,1)}), bf16[8,4,256,256]{3,2,1,0:T(8,128)(2,1)}, u32[]{:S(2)}, u32[]{:S(2)}) %all-to-all-start.1) | async-done | bytes 4194336 | tf_op jit(solution)/shard_map/all_to_all | solution.py:234
  126.3 3.6 %all-to-all-start.3 = ((s32[4,1,256]{2,1,0:T(1,128)}), s32[4,1,256]{2,1,0:T(1,128)S(1)}, u32[]{:S(2)}, u32[]{:S(2)}) async-start(s32[4,1,256]{2,1,0:T(1,128)} %reshape.38), calls=%async_computation.3 | async-start | bytes 8192 | tf_op jit(solution)/shard_map/all_to_all | solution.py:203
  130.0 12.3 %classes.1 = bf16[4,25,128,256]{3,2,1,0:T(8,128)(2,1)} custom-call(s32[128]{0:T(128)S(1)} %reshape_squeeze.9.labels, s32[1]{0:T(128)} %bitcast.3.block, bf16[32,256,256]{2,1,0:T(8,128)(2,1)} %bitcast.7.slots, bf16[512,256]{1,0:T(8,128)(2,1)S(1)} %copy-done.3), custom_call_target="tpu_custom_call" | custom-call | tf_op jit(solution)/shard_map/classes/pallas_call | solution.py:258
  142.3 5.4 %all-to-all-start.2 = ((bf16[4,25,128,256]{3,2,1,0:T(8,128)(2,1)}), bf16[4,25,128,256]{3,2,1,0:T(8,128)(2,1)}, u32[]{:S(2)}, u32[]{:S(2)}) async-start(bf16[4,25,128,256]{3,2,1,0:T(8,128)(2,1)} %classes.1), calls=%async_computation.2 | async-start | bytes 13107200 | tf_op jit(solution)/shard_map/all_to_all | solution.py:279
  147.8 0.5 broadcast.34
  148.3 0.7 reduce.12
  149.0 0.1 reshape.39
  149.1 0.1 slice_reduce_fusion
  149.4 16.4 %weights.1.weight = f32[25,64,256]{2,1,0:T(8,128)S(1)} custom-call(s32[512]{0:T(512)S(1)} %reshape_squeeze.10.labels, s32[512]{0:T(512)S(1)} %reshape_squeeze.11.groups, s32[1]{0:T(128)} %bitcast.3.block, f32[64]{0:T(128)S(1)} %copy-done.6, f32[64,256]{1,0:T(8,128)S(1)} %broadcast_add_fusion.radius), custom_call_target="tpu_custom_call" | custom-call | flops 41943040 | bytes 2097152 | tf_op jit(solution)/shard_map/weights/pallas_call | solution.py:244
  165.8 54.5 %all-to-all-done.2.received = bf16[4,25,128,256]{3,2,1,0:T(8,128)(2,1)} async-done(((bf16[4,25,128,256]{3,2,1,0:T(8,128)(2,1)}), bf16[4,25,128,256]{3,2,1,0:T(8,128)(2,1)}, u32[]{:S(2)}, u32[]{:S(2)}) %all-to-all-start.2) | async-done | bytes 6553632 | tf_op jit(solution)/shard_map/all_to_all | solution.py:279
  220.3 6.9 %finish.1 = f32[25,2,64,256]{3,2,1,0:T(8,128)} custom-call(bf16[4,25,128,256]{3,2,1,0:T(8,128)(2,1)} %all-to-all-done.2.received, f32[25,64,256]{2,1,0:T(8,128)S(1)} %weights.1.weight, bf16[256,512]{1,0:T(8,128)(2,1)S(1)} %copy-done.2), custom_call_target="tpu_custom_call" | custom-call | tf_op jit(solution)/shard_map/finish/pallas_call | solution.py:281
  (22 shorter events, 0.5 us)
Async XLA Ops:
  2.9 24.1 %all-to-all-start = ((s32[8,2,16]{2,1,0:T(2,128)}), s32[8,2,16]{2,1,0:T(2,128)S(1)}, u32[]{:S(2)}, u32[]{:S(2)}) async-start(s32[8,2,16]{2,1,0:T(2,128)} %broadcast_in_dim.6), calls=%async_computation | async-start | bytes 16384 | tf_op jit(solution)/shard_map/all_to_all | solution.py:200
  10.0 1.7 copy-start
  11.6 1.6 copy-start.1
  13.2 0.9 copy-start.4
  14.2 0.7 copy-start.5
  26.9 103.1 %copy-start.3 = (bf16[512,256]{1,0:T(8,128)(2,1)S(1)}, bf16[512,256]{1,0:T(8,128)(2,1)}, u32[]{:S(2)}) copy-start(bf16[512,256]{1,0:T(8,128)(2,1)} %constant.38.clone.expand) | copy-start | bytes 786436
  26.9 99.3 %all-to-all-start.1 = ((bf16[8,4,256,256]{3,2,1,0:T(8,128)(2,1)}), bf16[8,4,256,256]{3,2,1,0:T(8,128)(2,1)}, u32[]{:S(2)}, u32[]{:S(2)}) async-start(bf16[8,4,256,256]{3,2,1,0:T(8,128)(2,1)} %bitcast.11), calls=%async_computation.1 | async-start | bytes 8388608 | tf_op jit(solution)/shard_map/all_to_all | solution.py:234
  126.3 16.0 %all-to-all-start.3 = ((s32[4,1,256]{2,1,0:T(1,128)}), s32[4,1,256]{2,1,0:T(1,128)S(1)}, u32[]{:S(2)}, u32[]{:S(2)}) async-start(s32[4,1,256]{2,1,0:T(1,128)} %reshape.38), calls=%async_computation.3 | async-start | bytes 8192 | tf_op jit(solution)/shard_map/all_to_all | solution.py:203
  142.3 5.5 %copy-start.7 = (f32[256]{0:T(256)S(1)}, f32[256]{0:T(256)}, u32[]{:S(2)}) copy-start(f32[256]{0:T(256)} %constant.46) | copy-start | bytes 3076
  142.3 7.1 %copy-start.6 = (f32[64]{0:T(128)S(1)}, f32[64]{0:T(128)}, u32[]{:S(2)}) copy-start(f32[64]{0:T(128)} %defocus.3) | copy-start | bytes 772
  142.3 78.0 %copy-start.2 = (bf16[256,512]{1,0:T(8,128)(2,1)S(1)}, bf16[256,512]{1,0:T(8,128)(2,1)}, u32[]{:S(2)}) copy-start(bf16[256,512]{1,0:T(8,128)(2,1)} %constant.39.clone.expand) | copy-start | bytes 786436
  142.3 78.0 %all-to-all-start.2 = ((bf16[4,25,128,256]{3,2,1,0:T(8,128)(2,1)}), bf16[4,25,128,256]{3,2,1,0:T(8,128)(2,1)}, u32[]{:S(2)}, u32[]{:S(2)}) async-start(bf16[4,25,128,256]{3,2,1,0:T(8,128)(2,1)} %classes.1), calls=%async_computation.2 | async-start | bytes 13107200 | tf_op jit(solution)/shard_map/all_to_all | solution.py:279

commit v3 on v2

--- a/solution.py
+++ b/solution.py
@@ -77,7 +77,7 @@
     return out.reshape(extent, 2 * extent).astype(ml_dtypes.bfloat16)
 
 
-def transform_kernel(slot, info, defocus, image, rows, columns, radius, out, turned):
+def transform_kernel(slot, info, defocus, image, rows, columns, radius, low, high, turned):
     particle = pl.program_id(0)
     extent = image.shape[-1]
     turn = info[particle, 0]
@@ -109,10 +109,13 @@
     sign_y = jnp.where(flip_y, -1.0, 1.0)
     sign_x = jnp.where(flip_x, -1.0, 1.0)
     signs = jnp.where(row_sine, sign_y, 1.0) * jnp.where(column_sine, sign_x, 1.0)
-    out[0] = (spectrum * (contrast * signs)).astype(jnp.bfloat16)
-
-
-def class_kernel(sources, capacity, number, per_step, labels, block, slots, expand, out, total):
+    weighted = (spectrum * (contrast * signs)).astype(jnp.bfloat16)
+    low[0] = weighted[:, :half]
+    high[0] = weighted[:, half:]
+
+
+def class_kernel(sources, capacity, number, per_step, labels, block, slots, expand, *rest):
+    outs, total = rest[:-1], rest[-1]
     step = pl.program_id(0)
     loads = sources
 
@@ -137,13 +140,13 @@
 
     @pl.when(step >= loads)
     def _():
-        parts, _, double, extent = out.shape
+        _, double, _ = outs[0].shape
         for item in range(per_step):
             value = total[(step - loads) * per_step + item].astype(jnp.bfloat16)
             laid = jnp.dot(expand[...], value, preferred_element_type=jnp.float32)
             laid = laid.astype(jnp.bfloat16)
-            for part in range(parts):
-                out[part, item] = laid[part * double : (part + 1) * double]
+            for part, out in enumerate(outs):
+                out[item] = laid[part * double : (part + 1) * double]
 
 
 def weight_kernel(labels, groups, block, defocus, radius, out):
@@ -164,14 +167,18 @@
     lax.fori_loop(0, labels.shape[0], body, 0)
 
 
-def final_kernel(per_step, received, weight, expand, out):
-    parts = received.shape[0]
+def final_kernel(per_step, parts, *refs):
+    lows, highs, (weight, expand, out) = refs[:parts], refs[parts : 2 * parts], refs[2 * parts :]
     _, _, each, extent = out.shape
     for item in range(per_step):
-        value = received[0, item].astype(jnp.float32)
-        for part in range(1, parts):
-            value = value + received[part, item].astype(jnp.float32)
-        wide = jnp.dot(value.astype(jnp.bfloat16), expand[...], preferred_element_type=jnp.float32)
+        halves = []
+        for received in (lows, highs):
+            value = received[0][item].astype(jnp.float32)
+            for part in received[1:]:
+                value = value + part[item].astype(jnp.float32)
+            halves.append(value.astype(jnp.bfloat16))
+        value = jnp.concatenate(halves, axis=1)
+        wide = jnp.dot(value, expand[...], preferred_element_type=jnp.float32)
         inverse = 1.0 / (weight[item] + WIENER_TERM)
         out[item, 0] = (wide[:each, :extent] + wide[each:, extent:]) * inverse
         out[item, 1] = (wide[:each, extent:] - wide[each:, :extent]) * inverse
@@ -200,20 +207,14 @@
     column = lax.all_to_all(
         jnp.broadcast_to(own[None], (blocks, 2, number)), "cls", 0, 0, tiled=True
     )
-    labels = lax.all_to_all(
-        jnp.broadcast_to(column[None], (parts, blocks, 2, number)), "ptl", 0, 0, tiled=True
-    )
-    all_class = labels[:, :, 0].reshape(-1)
-    all_group = labels[:, :, 1].reshape(-1)
-    column_class = column[:, 0].reshape(-1)
-
     frequency, _ = packed(extent)
     share = (frequency / extent) ** 2
     packed_radius = (share[:, None] + share[None, :]).astype(np.float32)
     row_table, column_table = tables(extent)
 
     whole = lambda shape: pl.BlockSpec(shape, lambda *_: (0,) * len(shape))
-    outgoing = pl.pallas_call(
+    half = extent // 2
+    low, high = pl.pallas_call(
         transform_kernel,
         grid_spec=pltpu.PrefetchScalarGridSpec(
             num_scalar_prefetch=3,
@@ -224,16 +225,29 @@
                 whole(column_table.shape),
                 whole((extent, extent)),
             ],
-            out_specs=pl.BlockSpec((1, extent, extent), lambda i, slot, *_: (slot[i], 0, 0)),
+            out_specs=[pl.BlockSpec((1, extent, half), lambda i, slot, *_: (slot[i], 0, 0))] * 2,
             scratch_shapes=[pltpu.VMEM((extent, extent), jnp.bfloat16)],
         ),
-        out_shape=jax.ShapeDtypeStruct((blocks * capacity, extent, extent), jnp.bfloat16),
+        out_shape=[jax.ShapeDtypeStruct((blocks * capacity, extent, half), jnp.bfloat16)] * 2,
         compiler_params=params(),
         name="transform",
     )(slot, info, defocus, images, row_table, column_table, packed_radius)
-    arrived = lax.all_to_all(
-        outgoing.reshape(blocks, capacity, extent, extent), "cls", 0, 0, tiled=True
-    ).reshape(blocks * capacity, extent, extent)
+
+    def to_class(outgoing):
+        return lax.all_to_all(
+            outgoing.reshape(blocks, capacity, extent, half), "cls", 0, 0, tiled=True
+        ).reshape(blocks * capacity, extent, half)
+
+    low, column = lax.optimization_barrier((low, column))
+    labels = lax.all_to_all(
+        jnp.broadcast_to(column[None], (parts, blocks, 2, number)), "ptl", 0, 0, tiled=True
+    )
+    all_class = labels[:, :, 0].reshape(-1)
+    all_group = labels[:, :, 1].reshape(-1)
+    column_class = column[:, 0].reshape(-1)
+    low = to_class(low)
+    low, high, all_class, all_group = lax.optimization_barrier((low, high, all_class, all_group))
+    high = to_class(high)
 
     ky = part * each + jnp.arange(each, dtype=jnp.int32)
     kx = np.minimum(np.arange(extent), extent - np.arange(extent))
@@ -255,34 +269,52 @@
 
     per_step = 5
     steps = CLS_DEV // per_step
-    partial = pl.pallas_call(
-        functools.partial(class_kernel, blocks, capacity, number, per_step),
-        grid_spec=pltpu.PrefetchScalarGridSpec(
-            num_scalar_prefetch=2,
-            grid=(blocks + steps,),
-            in_specs=[
-                pl.BlockSpec(
-                    (capacity, extent, extent), lambda i, *_: (jnp.minimum(i, blocks - 1), 0, 0)
-                ),
-                whole((2 * extent, extent)),
-            ],
-            out_specs=pl.BlockSpec(
-                (parts, per_step, 2 * each, extent),
-                lambda i, *_: (0, jnp.maximum(i - blocks, 0), 0, 0),
+    expansion = jnp.roll(
+        jnp.asarray(row_expansion(extent, parts)).reshape(parts, 2 * each, extent), -part, axis=0
+    ).reshape(2 * extent, extent)
+
+    def class_sums(arrived):
+        sums = pl.pallas_call(
+            functools.partial(class_kernel, blocks, capacity, number, per_step),
+            grid_spec=pltpu.PrefetchScalarGridSpec(
+                num_scalar_prefetch=2,
+                grid=(blocks + steps,),
+                in_specs=[
+                    pl.BlockSpec(
+                        (capacity, extent, half), lambda i, *_: (jnp.minimum(i, blocks - 1), 0, 0)
+                    ),
+                    whole((2 * extent, extent)),
+                ],
+                out_specs=[
+                    pl.BlockSpec(
+                        (per_step, 2 * each, half), lambda i, *_: (jnp.maximum(i - blocks, 0), 0, 0)
+                    )
+                ]
+                * parts,
+                scratch_shapes=[pltpu.VMEM((CLS_DEV, extent, half), jnp.float32)],
             ),
-            scratch_shapes=[pltpu.VMEM((CLS_DEV, extent, extent), jnp.float32)],
-        ),
-        out_shape=jax.ShapeDtypeStruct((parts, CLS_DEV, 2 * each, extent), jnp.bfloat16),
-        compiler_params=params(),
-        name="classes",
-    )(column_class, me[None], arrived, row_expansion(extent, parts))
-    received = lax.all_to_all(partial, "ptl", 0, 0, tiled=True)
+            out_shape=[jax.ShapeDtypeStruct((CLS_DEV, 2 * each, half), jnp.bfloat16)] * parts,
+            compiler_params=params(),
+            cost_estimate=pl.CostEstimate(
+                flops=2 * CLS_DEV * 2 * extent * extent * half,
+                bytes_accessed=2**23,
+                transcendentals=0,
+            ),
+            name="classes",
+        )(column_class, me[None], arrived, expansion)
+        return [sums[0]] + [
+            lax.ppermute(sums[by], "ptl", [(q, (q + by) % parts) for q in range(parts)])
+            for by in range(1, parts)
+        ]
+
+    lows = class_sums(low)
+    highs = class_sums(high)
 
     return pl.pallas_call(
-        functools.partial(final_kernel, per_step),
+        functools.partial(final_kernel, per_step, parts),
         grid=(steps,),
-        in_specs=[
-            pl.BlockSpec((parts, per_step, 2 * each, extent), lambda i: (0, i, 0, 0)),
+        in_specs=[pl.BlockSpec((per_step, 2 * each, half), lambda i: (i, 0, 0))] * (2 * parts)
+        + [
             pl.BlockSpec((per_step, each, extent), lambda i: (i, 0, 0)),
             whole((extent, 2 * extent)),
         ],
@@ -290,7 +322,7 @@
         out_shape=jax.ShapeDtypeStruct((CLS_DEV, 2, each, extent), jnp.float32),
         compiler_params=params(),
         name="finish",
-    )(received, weight, column_expansion(extent))
+    )(*lows, *highs, weight, column_expansion(extent))
 
 
 def solution(mesh):

time: 228 us -> 201 us (0.88)
  waiting for transfers between devices: 148 us -> 101 us
  Pallas kernels: 47.7 us -> 57.2 us
  blocking collectives: 0 us -> 8.29 us
    all_to_all x3 -> x2, waiting for transfers between devices: 148 us -> 84.6 us  [to_class(): lax.all_to_all(outgoing.reshape(blocks, capacity, extent, half), 'cls', 0...]
    ppermute x0 -> x6, waiting for transfers between devices: none -> 16.8 us  [class_sums(): lax.ppermute(sums[by], 'ptl', [(q, (q + by) % parts) for q in range(parts)])]
    all_to_all x0 -> x1, blocking collectives: none -> 8.29 us  [per_device(): lax.all_to_all(jnp.broadcast_to(column[None], (parts, blocks, 2, number))...]
    ppermute x0 -> x6, starting transfers between devices: none -> 6.75 us  [class_sums(): lax.ppermute(sums[by], 'ptl', [(q, (q + by) % parts) for q in range(parts)])]
    pallas_call x2 -> x3, Pallas kernels: 19.1 us -> 25.7 us  [the longest x2 18.9 us: class_sums(): pl.pallas_call(functools.partial(class_kernel, blocks, capacity, number,...]
    all_to_all x3 -> x2, starting transfers between devices: 14.3 us -> 9.42 us  [to_class(): lax.all_to_all(outgoing.reshape(blocks, capacity, extent, half), 'cls', 0...]
    pallas_call x1, Pallas kernels: 12.1 us -> 15.1 us  [per_device(): pl.pallas_call(transform_kernel, grid_spec=pltpu.PrefetchScalarGridSpec(n...]
    unnamed x18 -> x22, local copies, waits for them, and re-layouts: 5.68 us -> 5.31 us
  transfers between devices with their start and end apart: 4 -> 9, of which waited for: 2 -> 4; matrix products, arithmetic and copies ran while one was open for 1% -> 1% of each run, Pallas kernels for 18% -> 25%
where the time goes in v3:
time: 201 us; the launch traced here: 200 us
  waiting for transfers between devices  101 us (50%)
  Pallas kernels  57.2 us (28%)
  starting transfers between devices  22.5 us (11%)
  blocking collectives  8.29 us (4%)
  local copies, waits for them, and re-layouts  6.85 us (3%)
  other arithmetic  3.6 us (2%)
    all_to_all x2, waiting for transfers between devices, to_class(): lax.all_to_all(outgoing.reshape(blocks, capacity, extent, half), 'cls', 0...  84.6 us
    pallas_call x2, Pallas kernels, class_sums(): pl.pallas_call(functools.partial(class_kernel, blocks, capacity, number,...  18.9 us
    ppermute x6, waiting for transfers between devices, class_sums(): lax.ppermute(sums[by], 'ptl', [(q, (q + by) % parts) for q in range(parts)])  16.8 us
    pallas_call x1, Pallas kernels, per_device(): pl.pallas_call(weight_kernel, in_specs=[smem, smem, smem, smem, vmem], ou...  16.4 us
    pallas_call x1, Pallas kernels, per_device(): pl.pallas_call(transform_kernel, grid_spec=pltpu.PrefetchScalarGridSpec(n...  15.1 us
    all_to_all x2, starting transfers between devices, to_class(): lax.all_to_all(outgoing.reshape(blocks, capacity, extent, half), 'cls', 0...  9.42 us
    all_to_all x1, blocking collectives, per_device(): lax.all_to_all(jnp.broadcast_to(column[None], (parts, blocks, 2, number))...  8.29 us
    pallas_call x1, Pallas kernels, per_device(): pl.pallas_call(functools.partial(final_kernel, per_step, parts), grid=(st...  6.77 us
  transfers between devices with their start and end apart: 9, of which 4 were waited for; matrix products, arithmetic and copies ran while one was open for 1% of the time, Pallas kernels for 25%

profile of v3, /device:TPU:0, one launch (start us, length us, event | category | flops | bytes accessed | tf_op | source)
XLA Modules:
  0.0 200.0 jit_solution(2502894541000181874)
XLA Ops:
  0.0 0.9 convert_reduce_fusion
  0.9 0.7 add_bitcast_fusion
  1.6 0.7 pad_add_fusion.1
  2.9 6.3 %all-to-all-start = ((s32[8,2,16]{2,1,0:T(2,128)}), s32[8,2,16]{2,1,0:T(2,128)S(1)}, u32[]{:S(2)}, u32[]{:S(2)}) async-start(s32[8,2,16]{2,1,0:T(2,128)} %broadcast_in_dim.6), calls=%async_computation | async-start | bytes 16384 | tf_op jit(solution)/shard_map/all_to_all | solution.py:207
  9.2 0.7 pad_add_fusion
  10.0 0.9 copy-done.5
  10.9 0.7 copy-done.6
  11.6 15.1 %transform.1 = (bf16[32,256,128]{2,1,0:T(8,128)(2,1)S(1)}, bf16[32,256,128]{2,1,0:T(8,128)(2,1)}) custom-call(s32[16]{0:T(128)S(1)} %get-tuple-element.40.slot, s32[16,4]{1,0:T(8,128)S(1)} %copy.19.info, f32[64]{0:T(128)S(1)} %copy-done.6, bf16[16,256,256]{2,1,0:T(8,128)(2,1)} %image.1, bf16[18,256,256]{2,1,0:T(8,128)(2,1)} %constant.54.clone.rows, ...), custom_call_target="tpu_custom_call" | custom-call | tf_op jit(solution)/shard_map/transform/pallas_call | solution.py:217
  26.7 1.3 copy-done.1
  28.1 8.3 %all_to_all.20 = s32[4,1,256]{2,1,0:T(1,128)S(1)} all-to-all(s32[4,1,256]{2,1,0:T(1,128)S(1)} %reshape.54), channel_id=1, replica_groups=mesh['cls'=8,'ptl'=4] {'ptl'}, dimensions={0} | all-to-all | bytes 8192 | tf_op jit(solution)/shard_map/all_to_all | solution.py:242
  36.4 4.9 %all-to-all-start.1 = ((bf16[8,4,256,128]{3,2,1,0:T(8,128)(2,1)}), bf16[8,4,256,128]{3,2,1,0:T(8,128)(2,1)S(1)}, u32[]{:S(2)}, u32[]{:S(2)}) async-start(bf16[8,4,256,128]{3,2,1,0:T(8,128)(2,1)} %bitcast.15), calls=%async_computation.1 | async-start | bytes 4194304 | tf_op jit(solution)/shard_map/all_to_all | solution.py:237
  42.8 47.6 %all-to-all-done.1 = bf16[8,4,256,128]{3,2,1,0:T(8,128)(2,1)S(1)} async-done(((bf16[8,4,256,128]{3,2,1,0:T(8,128)(2,1)}), bf16[8,4,256,128]{3,2,1,0:T(8,128)(2,1)S(1)}, u32[]{:S(2)}, u32[]{:S(2)}) %all-to-all-start.1) | async-done | bytes 2097184 | tf_op jit(solution)/shard_map/all_to_all | solution.py:237
  90.4 4.5 %all-to-all-start.3 = ((bf16[8,4,256,128]{3,2,1,0:T(8,128)(2,1)}), bf16[8,4,256,128]{3,2,1,0:T(8,128)(2,1)}, u32[]{:S(2)}, u32[]{:S(2)}) async-start(bf16[8,4,256,128]{3,2,1,0:T(8,128)(2,1)} %bitcast.9), calls=%async_computation.3 | async-start | bytes 4194304 | tf_op jit(solution)/shard_map/all_to_all | solution.py:237
  95.1 8.5 %classes.2 = (bf16[25,128,128]{2,1,0:T(8,128)(2,1)S(1)}, bf16[25,128,128]{2,1,0:T(8,128)(2,1)}, bf16[25,128,128]{2,1,0:T(8,128)(2,1)}, bf16[25,128,128]{2,1,0:T(8,128)(2,1)}) custom-call(s32[128]{0:T(128)S(1)} %reshape_squeeze.9.labels, s32[1]{0:T(128)} %bitcast.5.block, bf16[32,256,128]{2,1,0:T(8,128)(2,1)S(1)} %bitcast.14, bf16[512,256]{1,0:T(8,128)(2,1)S(1)} %bitcast.16), custom_call_target="tpu_custom_call" | custom-call | flops 838860800 | bytes 8388608 | tf_op jit(solution)/shard_map/classes/pallas_call | solution.py:277
  104.7 2.4 %collective-permute-start.2 = (bf16[25,128,128]{2,1,0:T(8,128)(2,1)}, bf16[25,128,128]{2,1,0:T(8,128)(2,1)}, u32[]{:S(2)}, u32[]{:S(2)}) collective-permute-start(bf16[25,128,128]{2,1,0:T(8,128)(2,1)} %get-tuple-element.29), channel_id=1, source_target_pairs={{0,3},{1,0},{2,1},{3,2},{4,7},{5,4},{6,5},{7,6},{8,11},{9,8},{10,9... | collective-permute-start | bytes 2457608 | tf_op jit(solution)/shard_map/ppermute | solution.py:306
  107.0 36.9 %all-to-all-done.3 = bf16[8,4,256,128]{3,2,1,0:T(8,128)(2,1)} async-done(((bf16[8,4,256,128]{3,2,1,0:T(8,128)(2,1)}), bf16[8,4,256,128]{3,2,1,0:T(8,128)(2,1)}, u32[]{:S(2)}, u32[]{:S(2)}) %all-to-all-start.3) | async-done | bytes 2097184 | tf_op jit(solution)/shard_map/all_to_all | solution.py:237
  144.0 10.5 %classes.3 = (bf16[25,128,128]{2,1,0:T(8,128)(2,1)S(1)}, bf16[25,128,128]{2,1,0:T(8,128)(2,1)}, bf16[25,128,128]{2,1,0:T(8,128)(2,1)}, bf16[25,128,128]{2,1,0:T(8,128)(2,1)}) custom-call(s32[128]{0:T(128)S(1)} %reshape_squeeze.9.labels, s32[1]{0:T(128)} %bitcast.5.block, bf16[32,256,128]{2,1,0:T(8,128)(2,1)} %bitcast.10.slots, bf16[512,256]{1,0:T(8,128)(2,1)S(1)} %bitcast.17), custom_call_target="tpu_custom_call" | custom-call | flops 838860800 | bytes 8388608 | tf_op jit(solution)/shard_map/classes/pallas_call | solution.py:277
  154.4 0.9 copy-done.2
  156.5 2.1 %collective-permute-start.5 = (bf16[25,128,128]{2,1,0:T(8,128)(2,1)}, bf16[25,128,128]{2,1,0:T(8,128)(2,1)}, u32[]{:S(2)}, u32[]{:S(2)}) collective-permute-start(bf16[25,128,128]{2,1,0:T(8,128)(2,1)} %get-tuple-element.34), channel_id=1, source_target_pairs={{0,3},{1,0},{2,1},{3,2},{4,7},{5,4},{6,5},{7,6},{8,11},{9,8},{10,9... | collective-permute-start | bytes 2457608 | tf_op jit(solution)/shard_map/ppermute | solution.py:306
  158.7 16.4 %weights.1.refs_8_ = f32[25,64,256]{2,1,0:T(8,128)S(1)} custom-call(s32[512]{0:T(512)S(1)} %reshape_squeeze.10.labels, s32[512]{0:T(512)S(1)} %reshape_squeeze.11.groups, s32[1]{0:T(128)} %bitcast.5.block, f32[64]{0:T(128)S(1)} %copy-done.7, f32[64,256]{1,0:T(8,128)S(1)} %broadcast_add_fusion.radius), custom_call_target="tpu_custom_call" | custom-call | flops 41943040 | bytes 2097152 | tf_op jit(solution)/shard_map/weights/pallas_call | solution.py:258
  175.1 1.2 copy-done
  176.4 1.3 collective-permute-done.3.refs_5_
  177.7 15.5 %collective-permute-done.4.refs_6_ = bf16[25,128,128]{2,1,0:T(8,128)(2,1)} collective-permute-done((bf16[25,128,128]{2,1,0:T(8,128)(2,1)}, bf16[25,128,128]{2,1,0:T(8,128)(2,1)}, u32[]{:S(2)}, u32[]{:S(2)}) %collective-permute-start.4) | collective-permute-done | bytes 819232 | tf_op jit(solution)/shard_map/ppermute | solution.py:306
  193.2 6.8 %finish.1 = f32[25,2,64,256]{3,2,1,0:T(8,128)} custom-call(bf16[25,128,128]{2,1,0:T(8,128)(2,1)S(1)} %get-tuple-element.26.refs_0_, bf16[25,128,128]{2,1,0:T(8,128)(2,1)S(1)} %collective-permute-done.refs_1_, bf16[25,128,128]{2,1,0:T(8,128)(2,1)S(1)} %collective-permute-done.1.refs_2_, bf16[25,128,128]{2,1,0:T(8,128)(2,1)} %collective-permute-done.2.refs_3_, ...), custom_call_target="tpu_custom_call" | custom-call | tf_op jit(solution)/shard_map/finish/pallas_call | solution.py:313
  (39 shorter events, 4.8 us)
Async XLA Ops:
  2.9 25.1 %all-to-all-start = ((s32[8,2,16]{2,1,0:T(2,128)}), s32[8,2,16]{2,1,0:T(2,128)S(1)}, u32[]{:S(2)}, u32[]{:S(2)}) async-start(s32[8,2,16]{2,1,0:T(2,128)} %broadcast_in_dim.6), calls=%async_computation | async-start | bytes 16384 | tf_op jit(solution)/shard_map/all_to_all | solution.py:207
  10.0 0.9 copy-start.5
  10.9 0.7 copy-start.6
  26.7 1.3 copy-start.1
  36.4 54.0 %all-to-all-start.1 = ((bf16[8,4,256,128]{3,2,1,0:T(8,128)(2,1)}), bf16[8,4,256,128]{3,2,1,0:T(8,128)(2,1)S(1)}, u32[]{:S(2)}, u32[]{:S(2)}) async-start(bf16[8,4,256,128]{3,2,1,0:T(8,128)(2,1)} %bitcast.15), calls=%async_computation.1 | async-start | bytes 4194304 | tf_op jit(solution)/shard_map/all_to_all | solution.py:237
  90.4 4.5 %copy-start.8 = (bf16[8,128,256]{2,1,0:T(8,128)(2,1)S(1)}, bf16[8,128,256]{2,1,0:T(8,128)(2,1)}, u32[]{:S(2)}) copy-start(bf16[8,128,256]{2,1,0:T(8,128)(2,1)} %constant.67) | copy-start | bytes 1572868
  90.4 53.6 %all-to-all-start.3 = ((bf16[8,4,256,128]{3,2,1,0:T(8,128)(2,1)}), bf16[8,4,256,128]{3,2,1,0:T(8,128)(2,1)}, u32[]{:S(2)}, u32[]{:S(2)}) async-start(bf16[8,4,256,128]{3,2,1,0:T(8,128)(2,1)} %bitcast.9), calls=%async_computation.3 | async-start | bytes 4194304 | tf_op jit(solution)/shard_map/all_to_all | solution.py:237
  103.5 55.1 %copy-start.9 = (f32[256]{0:T(256)S(1)}, f32[256]{0:T(256)}, u32[]{:S(2)}) copy-start(f32[256]{0:T(256)} %constant.68) | copy-start | bytes 3076
  103.5 55.1 %copy-start.7 = (f32[64]{0:T(128)S(1)}, f32[64]{0:T(128)}, u32[]{:S(2)}) copy-start(f32[64]{0:T(128)} %defocus.3) | copy-start | bytes 772
  103.5 53.0 %collective-permute-start = (bf16[25,128,128]{2,1,0:T(8,128)(2,1)}, bf16[25,128,128]{2,1,0:T(8,128)(2,1)S(1)}, u32[]{:S(2)}, u32[]{:S(2)}) collective-permute-start(bf16[25,128,128]{2,1,0:T(8,128)(2,1)} %get-tuple-element.27), channel_id=1, source_target_pairs={{0,1},{1,2},{2,3},{3,0},{4,5},{5,6},{6,7},{7,4},{8,9},{9,10},{10,1... | collective-permute-start | bytes 2457608 | tf_op jit(solution)/shard_map/ppermute | solution.py:306
  104.1 72.3 %collective-permute-start.1 = (bf16[25,128,128]{2,1,0:T(8,128)(2,1)}, bf16[25,128,128]{2,1,0:T(8,128)(2,1)S(1)}, u32[]{:S(2)}, u32[]{:S(2)}) collective-permute-start(bf16[25,128,128]{2,1,0:T(8,128)(2,1)} %get-tuple-element.28), channel_id=1, source_target_pairs={{0,2},{1,3},{2,0},{3,1},{4,6},{5,7},{6,4},{7,5},{8,10},{9,11},{10,... | collective-permute-start | bytes 2457608 | tf_op jit(solution)/shard_map/ppermute | solution.py:306
  104.7 71.7 %collective-permute-start.2 = (bf16[25,128,128]{2,1,0:T(8,128)(2,1)}, bf16[25,128,128]{2,1,0:T(8,128)(2,1)}, u32[]{:S(2)}, u32[]{:S(2)}) collective-permute-start(bf16[25,128,128]{2,1,0:T(8,128)(2,1)} %get-tuple-element.29), channel_id=1, source_target_pairs={{0,3},{1,0},{2,1},{3,2},{4,7},{5,4},{6,5},{7,6},{8,11},{9,8},{10,9... | collective-permute-start | bytes 2457608 | tf_op jit(solution)/shard_map/ppermute | solution.py:306
  144.0 49.3 %copy-start.4 = (bf16[256,512]{1,0:T(8,128)(2,1)S(1)}, bf16[256,512]{1,0:T(8,128)(2,1)}, u32[]{:S(2)}) copy-start(bf16[256,512]{1,0:T(8,128)(2,1)} %constant.59.clone.refs_9_) | copy-start | bytes 786436
  154.4 0.9 copy-start.2
  155.3 22.4 %collective-permute-start.3 = (bf16[25,128,128]{2,1,0:T(8,128)(2,1)}, bf16[25,128,128]{2,1,0:T(8,128)(2,1)}, u32[]{:S(2)}, u32[]{:S(2)}) collective-permute-start(bf16[25,128,128]{2,1,0:T(8,128)(2,1)} %get-tuple-element.32), channel_id=1, source_target_pairs={{0,1},{1,2},{2,3},{3,0},{4,5},{5,6},{6,7},{7,4},{8,9},{9,10},{10,1... | collective-permute-start | bytes 2457608 | tf_op jit(solution)/shard_map/ppermute | solution.py:306
  156.0 37.2 %collective-permute-start.4 = (bf16[25,128,128]{2,1,0:T(8,128)(2,1)}, bf16[25,128,128]{2,1,0:T(8,128)(2,1)}, u32[]{:S(2)}, u32[]{:S(2)}) collective-permute-start(bf16[25,128,128]{2,1,0:T(8,128)(2,1)} %get-tuple-element.33), channel_id=1, source_target_pairs={{0,2},{1,3},{2,0},{3,1},{4,6},{5,7},{6,4},{7,5},{8,10},{9,11},{10,... | collective-permute-start | bytes 2457608 | tf_op jit(solution)/shard_map/ppermute | solution.py:306
  156.5 36.7 %collective-permute-start.5 = (bf16[25,128,128]{2,1,0:T(8,128)(2,1)}, bf16[25,128,128]{2,1,0:T(8,128)(2,1)}, u32[]{:S(2)}, u32[]{:S(2)}) collective-permute-start(bf16[25,128,128]{2,1,0:T(8,128)(2,1)} %get-tuple-element.34), channel_id=1, source_target_pairs={{0,3},{1,0},{2,1},{3,2},{4,7},{5,4},{6,5},{7,6},{8,11},{9,8},{10,9... | collective-permute-start | bytes 2457608 | tf_op jit(solution)/shard_map/ppermute | solution.py:306
  158.6 34.6 %copy-start.3 = (bf16[25,128,128]{2,1,0:T(8,128)(2,1)S(1)}, bf16[25,128,128]{2,1,0:T(8,128)(2,1)}, u32[]{:S(2)}) copy-start(bf16[25,128,128]{2,1,0:T(8,128)(2,1)} %copy-done.2) | copy-start | bytes 2457604
  175.1 1.2 copy-start

commit v4 on v3

--- a/solution.py
+++ b/solution.py
@@ -239,14 +239,18 @@
         ).reshape(blocks * capacity, extent, half)
 
     low, column = lax.optimization_barrier((low, column))
-    labels = lax.all_to_all(
-        jnp.broadcast_to(column[None], (parts, blocks, 2, number)), "ptl", 0, 0, tiled=True
+    labels = jnp.stack(
+        [column]
+        + [
+            lax.ppermute(column, "ptl", [(q, (q + by) % parts) for q in range(parts)])
+            for by in range(1, parts)
+        ]
     )
     all_class = labels[:, :, 0].reshape(-1)
     all_group = labels[:, :, 1].reshape(-1)
     column_class = column[:, 0].reshape(-1)
     low = to_class(low)
-    low, high, all_class, all_group = lax.optimization_barrier((low, high, all_class, all_group))
+    low, high = lax.optimization_barrier((low, high))
     high = to_class(high)
 
     ky = part * each + jnp.arange(each, dtype=jnp.int32)

time: 201 us -> 206 us (1.025)
  blocking collectives: 8.29 us -> 54.1 us
  waiting for transfers between devices: 101 us -> 66.4 us
  Pallas kernels: 57.2 us -> 53.5 us
    all_to_all x2 -> x1, waiting for transfers between devices: 84.6 us -> 33.3 us  [to_class(): lax.all_to_all(outgoing.reshape(blocks, capacity, extent, half), 'cls', 0...]
    all_to_all x1, blocking collectives: 8.29 us -> 54.1 us  [to_class(): lax.all_to_all(outgoing.reshape(blocks, capacity, extent, half), 'cls', 0...]
    ppermute x6, waiting for transfers between devices: 16.8 us -> 33.1 us  [class_sums(): lax.ppermute(sums[by], 'ptl', [(q, (q + by) % parts) for q in range(parts)])]
    all_to_all x2 -> x1, starting transfers between devices: 9.42 us -> 3.74 us  [to_class(): lax.all_to_all(outgoing.reshape(blocks, capacity, extent, half), 'cls', 0...]
    ppermute x0 -> x3, starting transfers between devices: none -> 3.4 us  [per_device(): lax.ppermute(column, 'ptl', [(q, (q + by) % parts) for q in range(parts)])]
    pallas_call x2, Pallas kernels: 18.9 us -> 16.7 us  [class_sums(): pl.pallas_call(functools.partial(class_kernel, blocks, capacity, number,...]
    unnamed x22 -> x20, local copies, waits for them, and re-layouts: 5.31 us -> 5.29 us
  transfers between devices with their start and end apart: 9 -> 11, of which waited for: 4 -> 3; matrix products, arithmetic and copies ran while one was open for 1% -> 1% of each run, Pallas kernels for 25% -> 23%
where the time goes in v4:
time: 206 us; the launch traced here: 205 us
  waiting for transfers between devices  66.4 us (32%)
  blocking collectives  54.1 us (26%)
  Pallas kernels  53.5 us (26%)
  starting transfers between devices  21.4 us (10%)
  local copies, waits for them, and re-layouts  6.35 us (3%)
  other arithmetic  3.05 us (1%)
    all_to_all x1, blocking collectives, to_class(): lax.all_to_all(outgoing.reshape(blocks, capacity, extent, half), 'cls', 0...  54.1 us
    all_to_all x1, waiting for transfers between devices, to_class(): lax.all_to_all(outgoing.reshape(blocks, capacity, extent, half), 'cls', 0...  33.3 us
    ppermute x6, waiting for transfers between devices, class_sums(): lax.ppermute(sums[by], 'ptl', [(q, (q + by) % parts) for q in range(parts)])  33.1 us
    pallas_call x2, Pallas kernels, class_sums(): pl.pallas_call(functools.partial(class_kernel, blocks, capacity, number,...  16.7 us
    pallas_call x1, Pallas kernels, per_device(): pl.pallas_call(transform_kernel, grid_spec=pltpu.PrefetchScalarGridSpec(n...  15.1 us
    pallas_call x1, Pallas kernels, per_device(): pl.pallas_call(weight_kernel, in_specs=[smem, smem, smem, smem, vmem], ou...  14.8 us
    ppermute x6, starting transfers between devices, class_sums(): lax.ppermute(sums[by], 'ptl', [(q, (q + by) % parts) for q in range(parts)])  7.98 us
    pallas_call x1, Pallas kernels, per_device(): pl.pallas_call(functools.partial(final_kernel, per_step, parts), grid=(st...  6.88 us
  transfers between devices with their start and end apart: 11, of which 3 were waited for; matrix products, arithmetic and copies ran while one was open for 1% of the time, Pallas kernels for 23%

profile of v4, /device:TPU:0, one launch (start us, length us, event | category | flops | bytes accessed | tf_op | source)
XLA Modules:
  0.0 205.0 jit_solution(10992827657829219119)
XLA Ops:
  0.0 0.9 convert_reduce_fusion
  0.9 0.7 add_bitcast_fusion
  2.9 6.3 %all-to-all-start = ((s32[8,2,16]{2,1,0:T(2,128)}), s32[8,2,16]{2,1,0:T(2,128)S(1)}, u32[]{:S(2)}, u32[]{:S(2)}) async-start(s32[8,2,16]{2,1,0:T(2,128)} %broadcast_in_dim.4), calls=%async_computation | async-start | bytes 16384 | tf_op jit(solution)/shard_map/all_to_all | solution.py:207
  9.2 0.7 pad_add_fusion.1
  10.0 0.9 copy-done.5
  11.6 15.1 %transform.1 = (bf16[32,256,128]{2,1,0:T(8,128)(2,1)S(1)}, bf16[32,256,128]{2,1,0:T(8,128)(2,1)}) custom-call(s32[16]{0:T(128)S(1)} %get-tuple-element.36.slot, s32[16,4]{1,0:T(8,128)S(1)} %copy.18.info, f32[64]{0:T(128)S(1)} %copy-done.6, bf16[16,256,256]{2,1,0:T(8,128)(2,1)} %image.1, bf16[18,256,256]{2,1,0:T(8,128)(2,1)} %constant.54.clone.rows, ...), custom_call_target="tpu_custom_call" | custom-call | tf_op jit(solution)/shard_map/transform/pallas_call | solution.py:217
  26.7 54.1 %all_to_all.15 = bf16[8,4,256,128]{3,2,1,0:T(8,128)(2,1)} all-to-all(bf16[8,4,256,128]{3,2,1,0:T(8,128)(2,1)S(1)} %bitcast.20), channel_id=1, replica_groups=mesh['cls'=8,'ptl'=4] {'cls'}, dimensions={0} | all-to-all | bytes 4194304 | tf_op jit(solution)/shard_map/all_to_all | solution.py:237
  80.8 3.7 %all-to-all-start.2 = ((bf16[8,4,256,128]{3,2,1,0:T(8,128)(2,1)}), bf16[8,4,256,128]{3,2,1,0:T(8,128)(2,1)S(1)}, u32[]{:S(2)}, u32[]{:S(2)}) async-start(bf16[8,4,256,128]{3,2,1,0:T(8,128)(2,1)} %bitcast.9), calls=%async_computation.2 | async-start | bytes 4194304 | tf_op jit(solution)/shard_map/all_to_all | solution.py:237
  84.7 1.6 copy-done.1
  86.3 8.4 %classes.2 = (bf16[25,128,128]{2,1,0:T(8,128)(2,1)S(1)}, bf16[25,128,128]{2,1,0:T(8,128)(2,1)}, bf16[25,128,128]{2,1,0:T(8,128)(2,1)}, bf16[25,128,128]{2,1,0:T(8,128)(2,1)}) custom-call(s32[128]{0:T(128)S(1)} %reshape_squeeze.9.labels, s32[1]{0:T(128)} %bitcast.5.block, bf16[32,256,128]{2,1,0:T(8,128)(2,1)S(1)} %bitcast.19, bf16[512,256]{1,0:T(8,128)(2,1)S(1)} %bitcast.21), custom_call_target="tpu_custom_call" | custom-call | flops 838860800 | bytes 8388608 | tf_op jit(solution)/shard_map/classes/pallas_call | solution.py:281
  94.8 1.5 collective-permute-start
  96.2 1.5 collective-permute-start.8
  97.7 1.6 collective-permute-start.7
  100.3 33.3 %all-to-all-done.2 = bf16[8,4,256,128]{3,2,1,0:T(8,128)(2,1)S(1)} async-done(((bf16[8,4,256,128]{3,2,1,0:T(8,128)(2,1)}), bf16[8,4,256,128]{3,2,1,0:T(8,128)(2,1)S(1)}, u32[]{:S(2)}, u32[]{:S(2)}) %all-to-all-start.2) | async-done | bytes 2097184 | tf_op jit(solution)/shard_map/all_to_all | solution.py:237
  133.5 8.3 %classes.3 = (bf16[25,128,128]{2,1,0:T(8,128)(2,1)S(1)}, bf16[25,128,128]{2,1,0:T(8,128)(2,1)}, bf16[25,128,128]{2,1,0:T(8,128)(2,1)}, bf16[25,128,128]{2,1,0:T(8,128)(2,1)}) custom-call(s32[128]{0:T(128)S(1)} %reshape_squeeze.9.labels, s32[1]{0:T(128)} %bitcast.5.block, bf16[32,256,128]{2,1,0:T(8,128)(2,1)S(1)} %bitcast.18, bf16[512,256]{1,0:T(8,128)(2,1)S(1)} %bitcast.22), custom_call_target="tpu_custom_call" | custom-call | flops 838860800 | bytes 8388608 | tf_op jit(solution)/shard_map/classes/pallas_call | solution.py:281
  141.9 0.9 copy-done.2
  142.8 2.3 %collective-permute-start.2 = (bf16[25,128,128]{2,1,0:T(8,128)(2,1)}, bf16[25,128,128]{2,1,0:T(8,128)(2,1)S(1)}, u32[]{:S(2)}, u32[]{:S(2)}) collective-permute-start(bf16[25,128,128]{2,1,0:T(8,128)(2,1)} %get-tuple-element.27), channel_id=1, source_target_pairs={{0,3},{1,0},{2,1},{3,2},{4,7},{5,4},{6,5},{7,6},{8,11},{9,8},{10,9... | collective-permute-start | bytes 2457608 | tf_op jit(solution)/shard_map/ppermute | solution.py:310
  145.1 1.3 collective-permute-start.4
  146.4 2.2 %collective-permute-start.5 = (bf16[25,128,128]{2,1,0:T(8,128)(2,1)}, bf16[25,128,128]{2,1,0:T(8,128)(2,1)}, u32[]{:S(2)}, u32[]{:S(2)}) collective-permute-start(bf16[25,128,128]{2,1,0:T(8,128)(2,1)} %get-tuple-element.32), channel_id=1, source_target_pairs={{0,3},{1,0},{2,1},{3,2},{4,7},{5,4},{6,5},{7,6},{8,11},{9,8},{10,9... | collective-permute-start | bytes 2457608 | tf_op jit(solution)/shard_map/ppermute | solution.py:310
  149.0 14.8 %weights.1.refs_8_ = f32[25,64,256]{2,1,0:T(8,128)S(1)} custom-call(s32[512]{0:T(512)S(1)} %reshape_squeeze.10.labels, s32[512]{0:T(512)S(1)} %reshape_squeeze.11.groups, s32[1]{0:T(128)} %bitcast.5.block, f32[64]{0:T(128)S(1)} %copy-done.7, f32[64,256]{1,0:T(8,128)S(1)} %broadcast_add_fusion.radius), custom_call_target="tpu_custom_call" | custom-call | flops 41943040 | bytes 2097152 | tf_op jit(solution)/shard_map/weights/pallas_call | solution.py:262
  163.8 1.2 copy-done
  165.0 17.9 %collective-permute-done.3.refs_5_ = bf16[25,128,128]{2,1,0:T(8,128)(2,1)} collective-permute-done((bf16[25,128,128]{2,1,0:T(8,128)(2,1)}, bf16[25,128,128]{2,1,0:T(8,128)(2,1)}, u32[]{:S(2)}, u32[]{:S(2)}) %collective-permute-start.3) | collective-permute-done | bytes 819232 | tf_op jit(solution)/shard_map/ppermute | solution.py:310
  182.9 15.3 %collective-permute-done.5.refs_7_ = bf16[25,128,128]{2,1,0:T(8,128)(2,1)} collective-permute-done((bf16[25,128,128]{2,1,0:T(8,128)(2,1)}, bf16[25,128,128]{2,1,0:T(8,128)(2,1)}, u32[]{:S(2)}, u32[]{:S(2)}) %collective-permute-start.5) | collective-permute-done | bytes 819232 | tf_op jit(solution)/shard_map/ppermute | solution.py:310
  198.1 6.9 %finish.1 = f32[25,2,64,256]{3,2,1,0:T(8,128)} custom-call(bf16[25,128,128]{2,1,0:T(8,128)(2,1)S(1)} %get-tuple-element.24.refs_0_, bf16[25,128,128]{2,1,0:T(8,128)(2,1)} %collective-permute-done.refs_1_, bf16[25,128,128]{2,1,0:T(8,128)(2,1)} %collective-permute-done.1.refs_2_, bf16[25,128,128]{2,1,0:T(8,128)(2,1)S(1)} %collective-permute-done.2.refs_3_, ...), custom_call_target="tpu_custom_call" | custom-call | tf_op jit(solution)/shard_map/finish/pallas_call | solution.py:317
  (39 shorter events, 3.5 us)
Async XLA Ops:
  2.9 23.8 %all-to-all-start = ((s32[8,2,16]{2,1,0:T(2,128)}), s32[8,2,16]{2,1,0:T(2,128)S(1)}, u32[]{:S(2)}, u32[]{:S(2)}) async-start(s32[8,2,16]{2,1,0:T(2,128)} %broadcast_in_dim.4), calls=%async_computation | async-start | bytes 16384 | tf_op jit(solution)/shard_map/all_to_all | solution.py:207
  10.0 0.9 copy-start.5
  10.9 0.7 copy-start.6
  80.8 3.8 %copy-start.8 = (bf16[8,128,256]{2,1,0:T(8,128)(2,1)S(1)}, bf16[8,128,256]{2,1,0:T(8,128)(2,1)}, u32[]{:S(2)}) copy-start(bf16[8,128,256]{2,1,0:T(8,128)(2,1)} %constant.67) | copy-start | bytes 1572868
  80.8 52.7 %all-to-all-start.2 = ((bf16[8,4,256,128]{3,2,1,0:T(8,128)(2,1)}), bf16[8,4,256,128]{3,2,1,0:T(8,128)(2,1)S(1)}, u32[]{:S(2)}, u32[]{:S(2)}) async-start(bf16[8,4,256,128]{3,2,1,0:T(8,128)(2,1)} %bitcast.9), calls=%async_computation.2 | async-start | bytes 4194304 | tf_op jit(solution)/shard_map/all_to_all | solution.py:237
  84.7 1.6 copy-start.1
  94.7 53.9 %copy-start.9 = (f32[256]{0:T(256)S(1)}, f32[256]{0:T(256)}, u32[]{:S(2)}) copy-start(f32[256]{0:T(256)} %constant.68) | copy-start | bytes 3076
  94.8 54.2 %copy-start.7 = (f32[64]{0:T(128)S(1)}, f32[64]{0:T(128)}, u32[]{:S(2)}) copy-start(f32[64]{0:T(128)} %defocus.3) | copy-start | bytes 772
  94.8 51.6 %collective-permute-start = (bf16[25,128,128]{2,1,0:T(8,128)(2,1)}, bf16[25,128,128]{2,1,0:T(8,128)(2,1)}, u32[]{:S(2)}, u32[]{:S(2)}) collective-permute-start(bf16[25,128,128]{2,1,0:T(8,128)(2,1)} %get-tuple-element.25), channel_id=1, source_target_pairs={{0,1},{1,2},{2,3},{3,0},{4,5},{5,6},{6,7},{7,4},{8,9},{9,10},{10,1... | collective-permute-start | bytes 2457608 | tf_op jit(solution)/shard_map/ppermute | solution.py:310
  96.2 46.5 %collective-permute-start.8 = (s32[8,2,16]{2,1,0:T(2,128)S(1)}, s32[8,2,16]{2,1,0:T(2,128)S(1)}, u32[]{:S(2)}, u32[]{:S(2)}) collective-permute-start(s32[8,2,16]{2,1,0:T(2,128)S(1)} %all-to-all-done), channel_id=1, source_target_pairs={{0,3},{1,0},{2,1},{3,2},{4,7},{5,4},{6,5},{7,6},{8,11},{9,8},{10,9... | collective-permute-start | bytes 3080 | tf_op jit(solution)/shard_map/ppermute | solution.py:245
  97.7 47.4 %collective-permute-start.7 = (s32[8,2,16]{2,1,0:T(2,128)S(1)}, s32[8,2,16]{2,1,0:T(2,128)S(1)}, u32[]{:S(2)}, u32[]{:S(2)}) collective-permute-start(s32[8,2,16]{2,1,0:T(2,128)S(1)} %all-to-all-done), channel_id=1, source_target_pairs={{0,2},{1,3},{2,0},{3,1},{4,6},{5,7},{6,4},{7,5},{8,10},{9,11},{10,... | collective-permute-start | bytes 3080 | tf_op jit(solution)/shard_map/ppermute | solution.py:245
  99.3 45.8 %collective-permute-start.6 = (s32[8,2,16]{2,1,0:T(2,128)S(1)}, s32[8,2,16]{2,1,0:T(2,128)S(1)}, u32[]{:S(2)}, u32[]{:S(2)}) collective-permute-start(s32[8,2,16]{2,1,0:T(2,128)S(1)} %all-to-all-done), channel_id=1, source_target_pairs={{0,1},{1,2},{2,3},{3,0},{4,5},{5,6},{6,7},{7,4},{8,9},{9,10},{10,1... | collective-permute-start | bytes 3080 | tf_op jit(solution)/shard_map/ppermute | solution.py:245
  99.6 65.4 %collective-permute-start.1 = (bf16[25,128,128]{2,1,0:T(8,128)(2,1)}, bf16[25,128,128]{2,1,0:T(8,128)(2,1)}, u32[]{:S(2)}, u32[]{:S(2)}) collective-permute-start(bf16[25,128,128]{2,1,0:T(8,128)(2,1)} %get-tuple-element.26), channel_id=1, source_target_pairs={{0,2},{1,3},{2,0},{3,1},{4,6},{5,7},{6,4},{7,5},{8,10},{9,11},{10,... | collective-permute-start | bytes 2457608 | tf_op jit(solution)/shard_map/ppermute | solution.py:310
  133.5 64.6 %copy-start.4 = (bf16[256,512]{1,0:T(8,128)(2,1)S(1)}, bf16[256,512]{1,0:T(8,128)(2,1)}, u32[]{:S(2)}) copy-start(bf16[256,512]{1,0:T(8,128)(2,1)} %constant.59.clone.refs_9_) | copy-start | bytes 786436
  141.9 0.9 copy-start.2
  142.8 55.4 %copy-start.3 = (bf16[25,128,128]{2,1,0:T(8,128)(2,1)S(1)}, bf16[25,128,128]{2,1,0:T(8,128)(2,1)}, u32[]{:S(2)}) copy-start(bf16[25,128,128]{2,1,0:T(8,128)(2,1)} %copy-done.2) | copy-start | bytes 2457604
  142.8 22.2 %collective-permute-start.2 = (bf16[25,128,128]{2,1,0:T(8,128)(2,1)}, bf16[25,128,128]{2,1,0:T(8,128)(2,1)S(1)}, u32[]{:S(2)}, u32[]{:S(2)}) collective-permute-start(bf16[25,128,128]{2,1,0:T(8,128)(2,1)} %get-tuple-element.27), channel_id=1, source_target_pairs={{0,3},{1,0},{2,1},{3,2},{4,7},{5,4},{6,5},{7,6},{8,11},{9,8},{10,9... | collective-permute-start | bytes 2457608 | tf_op jit(solution)/shard_map/ppermute | solution.py:310
  145.0 37.8 %collective-permute-start.3 = (bf16[25,128,128]{2,1,0:T(8,128)(2,1)}, bf16[25,128,128]{2,1,0:T(8,128)(2,1)}, u32[]{:S(2)}, u32[]{:S(2)}) collective-permute-start(bf16[25,128,128]{2,1,0:T(8,128)(2,1)} %get-tuple-element.30), channel_id=1, source_target_pairs={{0,1},{1,2},{2,3},{3,0},{4,5},{5,6},{6,7},{7,4},{8,9},{9,10},{10,1... | collective-permute-start | bytes 2457608 | tf_op jit(solution)/shard_map/ppermute | solution.py:310
  145.1 37.8 %collective-permute-start.4 = (bf16[25,128,128]{2,1,0:T(8,128)(2,1)}, bf16[25,128,128]{2,1,0:T(8,128)(2,1)}, u32[]{:S(2)}, u32[]{:S(2)}) collective-permute-start(bf16[25,128,128]{2,1,0:T(8,128)(2,1)} %get-tuple-element.31), channel_id=1, source_target_pairs={{0,2},{1,3},{2,0},{3,1},{4,6},{5,7},{6,4},{7,5},{8,10},{9,11},{10,... | collective-permute-start | bytes 2457608 | tf_op jit(solution)/shard_map/ppermute | solution.py:310
  146.4 51.7 %collective-permute-start.5 = (bf16[25,128,128]{2,1,0:T(8,128)(2,1)}, bf16[25,128,128]{2,1,0:T(8,128)(2,1)}, u32[]{:S(2)}, u32[]{:S(2)}) collective-permute-start(bf16[25,128,128]{2,1,0:T(8,128)(2,1)} %get-tuple-element.32), channel_id=1, source_target_pairs={{0,3},{1,0},{2,1},{3,2},{4,7},{5,4},{6,5},{7,6},{8,11},{9,8},{10,9... | collective-permute-start | bytes 2457608 | tf_op jit(solution)/shard_map/ppermute | solution.py:310
  163.8 1.2 copy-start

commit v5 on v4

--- a/solution.py
+++ b/solution.py
@@ -250,7 +250,7 @@
     all_group = labels[:, :, 1].reshape(-1)
     column_class = column[:, 0].reshape(-1)
     low = to_class(low)
-    low, high = lax.optimization_barrier((low, high))
+    low, high, all_class, all_group = lax.optimization_barrier((low, high, all_class, all_group))
     high = to_class(high)
 
     ky = part * each + jnp.arange(each, dtype=jnp.int32)

time: 206 us -> 193 us (0.937)
  blocking collectives: 54.1 us -> 0 us
  waiting for transfers between devices: 66.4 us -> 98 us
  starting transfers between devices: 21.4 us -> 28 us
  Pallas kernels: 53.5 us -> 57.1 us
    all_to_all x1 -> x0, blocking collectives: 54.1 us -> none  [to_class(): lax.all_to_all(outgoing.reshape(blocks, capacity, extent, half), 'cls', 0...]
    all_to_all x1 -> x2, waiting for transfers between devices: 33.3 us -> 77.5 us  [to_class(): lax.all_to_all(outgoing.reshape(blocks, capacity, extent, half), 'cls', 0...]
    ppermute x6, waiting for transfers between devices: 33.1 us -> 16.3 us  [class_sums(): lax.ppermute(sums[by], 'ptl', [(q, (q + by) % parts) for q in range(parts)])]
    all_to_all x1 -> x2, starting transfers between devices: 3.74 us -> 9.71 us  [to_class(): lax.all_to_all(outgoing.reshape(blocks, capacity, extent, half), 'cls', 0...]
    ppermute x3, waiting for transfers between devices: 0.01 us -> 4.18 us  [per_device(): lax.ppermute(column, 'ptl', [(q, (q + by) % parts) for q in range(parts)])]
    pallas_call x2, Pallas kernels: 16.7 us -> 18.8 us  [class_sums(): pl.pallas_call(functools.partial(class_kernel, blocks, capacity, number,...]
  transfers between devices with their start and end apart: 11 -> 12, of which waited for: 3 -> 8; matrix products, arithmetic and copies ran while one was open for 1% -> 1% of each run, Pallas kernels for 23% -> 26%
where the time goes in v5:
time: 193 us; the launch traced here: 192 us
  waiting for transfers between devices  98 us (51%)
  Pallas kernels  57.1 us (30%)
  starting transfers between devices  28 us (15%)
  local copies, waits for them, and re-layouts  6.14 us (3%)
  other arithmetic  3.05 us (2%)
    all_to_all x2, waiting for transfers between devices, to_class(): lax.all_to_all(outgoing.reshape(blocks, capacity, extent, half), 'cls', 0...  77.5 us
    pallas_call x2, Pallas kernels, class_sums(): pl.pallas_call(functools.partial(class_kernel, blocks, capacity, number,...  18.8 us
    pallas_call x1, Pallas kernels, per_device(): pl.pallas_call(weight_kernel, in_specs=[smem, smem, smem, smem, vmem], ou...  16.4 us
    ppermute x6, waiting for transfers between devices, class_sums(): lax.ppermute(sums[by], 'ptl', [(q, (q + by) % parts) for q in range(parts)])  16.3 us
    pallas_call x1, Pallas kernels, per_device(): pl.pallas_call(transform_kernel, grid_spec=pltpu.PrefetchScalarGridSpec(n...  15 us
    all_to_all x2, starting transfers between devices, to_class(): lax.all_to_all(outgoing.reshape(blocks, capacity, extent, half), 'cls', 0...  9.71 us
    ppermute x6, starting transfers between devices, class_sums(): lax.ppermute(sums[by], 'ptl', [(q, (q + by) % parts) for q in range(parts)])  8.69 us
    pallas_call x1, Pallas kernels, per_device(): pl.pallas_call(functools.partial(final_kernel, per_step, parts), grid=(st...  6.77 us
  transfers between devices with their start and end apart: 12, of which 8 were waited for; matrix products, arithmetic and copies ran while one was open for 1% of the time, Pallas kernels for 26%

profile of v5, /device:TPU:0, one launch (start us, length us, event | category | flops | bytes accessed | tf_op | source)
XLA Modules:
  0.0 192.4 jit_solution(15549295813088329594)
XLA Ops:
  0.0 0.9 convert_reduce_fusion
  2.8 6.3 %all-to-all-start = ((s32[8,2,16]{2,1,0:T(2,128)}), s32[8,2,16]{2,1,0:T(2,128)S(1)}, u32[]{:S(2)}, u32[]{:S(2)}) async-start(s32[8,2,16]{2,1,0:T(2,128)} %broadcast_in_dim.4), calls=%async_computation | async-start | bytes 16384 | tf_op jit(solution)/shard_map/all_to_all | solution.py:207
  10.0 0.9 copy-done.5
  11.6 15.0 %transform.1 = (bf16[32,256,128]{2,1,0:T(8,128)(2,1)S(1)}, bf16[32,256,128]{2,1,0:T(8,128)(2,1)}) custom-call(s32[16]{0:T(128)S(1)} %get-tuple-element.40.slot, s32[16,4]{1,0:T(8,128)S(1)} %copy.18.info, f32[64]{0:T(128)S(1)} %copy-done.6, bf16[16,256,256]{2,1,0:T(8,128)(2,1)} %image.1, bf16[18,256,256]{2,1,0:T(8,128)(2,1)} %constant.54.clone.rows, ...), custom_call_target="tpu_custom_call" | custom-call | tf_op jit(solution)/shard_map/transform/pallas_call | solution.py:217
  26.6 1.3 copy-done.1
  27.9 5.2 %all-to-all-start.1 = ((bf16[8,4,256,128]{3,2,1,0:T(8,128)(2,1)}), bf16[8,4,256,128]{3,2,1,0:T(8,128)(2,1)S(1)}, u32[]{:S(2)}, u32[]{:S(2)}) async-start(bf16[8,4,256,128]{3,2,1,0:T(8,128)(2,1)} %bitcast.19), calls=%async_computation.1 | async-start | bytes 4194304 | tf_op jit(solution)/shard_map/all_to_all | solution.py:237
  33.2 2.5 %collective-permute-start.2 = (s32[8,2,16]{2,1,0:T(2,128)S(1)}, s32[8,2,16]{2,1,0:T(2,128)S(1)}, u32[]{:S(2)}, u32[]{:S(2)}) collective-permute-start(s32[8,2,16]{2,1,0:T(2,128)S(1)} %all-to-all-done), channel_id=1, source_target_pairs={{0,3},{1,0},{2,1},{3,2},{4,7},{5,4},{6,5},{7,6},{8,11},{9,8},{10,9... | collective-permute-start | bytes 3080 | tf_op jit(solution)/shard_map/ppermute | solution.py:245
  37.0 2.3 %collective-permute-done.1 = s32[8,2,16]{2,1,0:T(2,128)S(1)} collective-permute-done((s32[8,2,16]{2,1,0:T(2,128)S(1)}, s32[8,2,16]{2,1,0:T(2,128)S(1)}, u32[]{:S(2)}, u32[]{:S(2)}) %collective-permute-start.1) | collective-permute-done | bytes 1056 | tf_op jit(solution)/shard_map/ppermute | solution.py:245
  39.3 1.4 collective-permute-done
  40.9 41.3 %all-to-all-done.1 = bf16[8,4,256,128]{3,2,1,0:T(8,128)(2,1)S(1)} async-done(((bf16[8,4,256,128]{3,2,1,0:T(8,128)(2,1)}), bf16[8,4,256,128]{3,2,1,0:T(8,128)(2,1)S(1)}, u32[]{:S(2)}, u32[]{:S(2)}) %all-to-all-start.1) | async-done | bytes 2097184 | tf_op jit(solution)/shard_map/all_to_all | solution.py:237
  82.2 4.5 %all-to-all-start.2 = ((bf16[8,4,256,128]{3,2,1,0:T(8,128)(2,1)}), bf16[8,4,256,128]{3,2,1,0:T(8,128)(2,1)}, u32[]{:S(2)}, u32[]{:S(2)}) async-start(bf16[8,4,256,128]{3,2,1,0:T(8,128)(2,1)} %bitcast.13), calls=%async_computation.2 | async-start | bytes 4194304 | tf_op jit(solution)/shard_map/all_to_all | solution.py:237
  86.9 8.5 %classes.2 = (bf16[25,128,128]{2,1,0:T(8,128)(2,1)S(1)}, bf16[25,128,128]{2,1,0:T(8,128)(2,1)}, bf16[25,128,128]{2,1,0:T(8,128)(2,1)}, bf16[25,128,128]{2,1,0:T(8,128)(2,1)}) custom-call(s32[128]{0:T(128)S(1)} %reshape_squeeze.9.labels, s32[1]{0:T(128)} %bitcast.5.block, bf16[32,256,128]{2,1,0:T(8,128)(2,1)S(1)} %bitcast.18, bf16[512,256]{1,0:T(8,128)(2,1)S(1)} %bitcast.20), custom_call_target="tpu_custom_call" | custom-call | flops 838860800 | bytes 8388608 | tf_op jit(solution)/shard_map/classes/pallas_call | solution.py:281
  95.4 1.5 collective-permute-start.3
  96.9 1.5 collective-permute-start.4
  98.4 1.2 collective-permute-start.5
  99.6 36.2 %all-to-all-done.2 = bf16[8,4,256,128]{3,2,1,0:T(8,128)(2,1)} async-done(((bf16[8,4,256,128]{3,2,1,0:T(8,128)(2,1)}), bf16[8,4,256,128]{3,2,1,0:T(8,128)(2,1)}, u32[]{:S(2)}, u32[]{:S(2)}) %all-to-all-start.2) | async-done | bytes 2097184 | tf_op jit(solution)/shard_map/all_to_all | solution.py:237
  135.8 10.3 %classes.3 = (bf16[25,128,128]{2,1,0:T(8,128)(2,1)S(1)}, bf16[25,128,128]{2,1,0:T(8,128)(2,1)}, bf16[25,128,128]{2,1,0:T(8,128)(2,1)}, bf16[25,128,128]{2,1,0:T(8,128)(2,1)}) custom-call(s32[128]{0:T(128)S(1)} %reshape_squeeze.9.labels, s32[1]{0:T(128)} %bitcast.5.block, bf16[32,256,128]{2,1,0:T(8,128)(2,1)} %bitcast.14.slots, bf16[512,256]{1,0:T(8,128)(2,1)S(1)} %bitcast.21), custom_call_target="tpu_custom_call" | custom-call | flops 838860800 | bytes 8388608 | tf_op jit(solution)/shard_map/classes/pallas_call | solution.py:281
  147.0 1.4 collective-permute-start.6
  148.4 1.9 collective-permute-start.7
  150.3 1.2 collective-permute-start.8
  151.6 16.4 %weights.1.refs_8_ = f32[25,64,256]{2,1,0:T(8,128)S(1)} custom-call(s32[512]{0:T(512)S(1)} %reshape_squeeze.10.labels, s32[512]{0:T(512)S(1)} %reshape_squeeze.11.groups, s32[1]{0:T(128)} %bitcast.5.block, f32[64]{0:T(128)S(1)} %copy-done.7, f32[64,256]{1,0:T(8,128)S(1)} %broadcast_add_fusion.radius), custom_call_target="tpu_custom_call" | custom-call | flops 41943040 | bytes 2097152 | tf_op jit(solution)/shard_map/weights/pallas_call | solution.py:262
  168.1 1.2 copy-done
  169.4 16.1 %collective-permute-done.7.refs_6_ = bf16[25,128,128]{2,1,0:T(8,128)(2,1)} collective-permute-done((bf16[25,128,128]{2,1,0:T(8,128)(2,1)}, bf16[25,128,128]{2,1,0:T(8,128)(2,1)}, u32[]{:S(2)}, u32[]{:S(2)}) %collective-permute-start.7) | collective-permute-done | bytes 819232 | tf_op jit(solution)/shard_map/ppermute | solution.py:310
  185.6 6.8 %finish.1 = f32[25,2,64,256]{3,2,1,0:T(8,128)} custom-call(bf16[25,128,128]{2,1,0:T(8,128)(2,1)S(1)} %get-tuple-element.26.refs_0_, bf16[25,128,128]{2,1,0:T(8,128)(2,1)S(1)} %collective-permute-done.3.refs_1_, bf16[25,128,128]{2,1,0:T(8,128)(2,1)S(1)} %collective-permute-done.4.refs_2_, bf16[25,128,128]{2,1,0:T(8,128)(2,1)} %collective-permute-done.5.refs_3_, ...), custom_call_target="tpu_custom_call" | custom-call | tf_op jit(solution)/shard_map/finish/pallas_call | solution.py:317
  (40 shorter events, 6.4 us)
Async XLA Ops:
  2.8 25.1 %all-to-all-start = ((s32[8,2,16]{2,1,0:T(2,128)}), s32[8,2,16]{2,1,0:T(2,128)S(1)}, u32[]{:S(2)}, u32[]{:S(2)}) async-start(s32[8,2,16]{2,1,0:T(2,128)} %broadcast_in_dim.4), calls=%async_computation | async-start | bytes 16384 | tf_op jit(solution)/shard_map/all_to_all | solution.py:207
  10.0 0.9 copy-start.5
  10.9 0.7 copy-start.6
  26.6 1.3 copy-start.1
  27.9 54.3 %all-to-all-start.1 = ((bf16[8,4,256,128]{3,2,1,0:T(8,128)(2,1)}), bf16[8,4,256,128]{3,2,1,0:T(8,128)(2,1)S(1)}, u32[]{:S(2)}, u32[]{:S(2)}) async-start(bf16[8,4,256,128]{3,2,1,0:T(8,128)(2,1)} %bitcast.19), calls=%async_computation.1 | async-start | bytes 4194304 | tf_op jit(solution)/shard_map/all_to_all | solution.py:237
  33.2 3.8 %collective-permute-start.2 = (s32[8,2,16]{2,1,0:T(2,128)S(1)}, s32[8,2,16]{2,1,0:T(2,128)S(1)}, u32[]{:S(2)}, u32[]{:S(2)}) collective-permute-start(s32[8,2,16]{2,1,0:T(2,128)S(1)} %all-to-all-done), channel_id=1, source_target_pairs={{0,3},{1,0},{2,1},{3,2},{4,7},{5,4},{6,5},{7,6},{8,11},{9,8},{10,9... | collective-permute-start | bytes 3080 | tf_op jit(solution)/shard_map/ppermute | solution.py:245
  35.6 3.7 %collective-permute-start.1 = (s32[8,2,16]{2,1,0:T(2,128)S(1)}, s32[8,2,16]{2,1,0:T(2,128)S(1)}, u32[]{:S(2)}, u32[]{:S(2)}) collective-permute-start(s32[8,2,16]{2,1,0:T(2,128)S(1)} %all-to-all-done), channel_id=1, source_target_pairs={{0,2},{1,3},{2,0},{3,1},{4,6},{5,7},{6,4},{7,5},{8,10},{9,11},{10,... | collective-permute-start | bytes 3080 | tf_op jit(solution)/shard_map/ppermute | solution.py:245
  36.1 4.5 %collective-permute-start = (s32[8,2,16]{2,1,0:T(2,128)S(1)}, s32[8,2,16]{2,1,0:T(2,128)S(1)}, u32[]{:S(2)}, u32[]{:S(2)}) collective-permute-start(s32[8,2,16]{2,1,0:T(2,128)S(1)} %all-to-all-done), channel_id=1, source_target_pairs={{0,1},{1,2},{2,3},{3,0},{4,5},{5,6},{6,7},{7,4},{8,9},{9,10},{10,1... | collective-permute-start | bytes 3080 | tf_op jit(solution)/shard_map/ppermute | solution.py:245
  82.2 4.5 %copy-start.8 = (bf16[8,128,256]{2,1,0:T(8,128)(2,1)S(1)}, bf16[8,128,256]{2,1,0:T(8,128)(2,1)}, u32[]{:S(2)}) copy-start(bf16[8,128,256]{2,1,0:T(8,128)(2,1)} %constant.67) | copy-start | bytes 1572868
  82.2 53.5 %all-to-all-start.2 = ((bf16[8,4,256,128]{3,2,1,0:T(8,128)(2,1)}), bf16[8,4,256,128]{3,2,1,0:T(8,128)(2,1)}, u32[]{:S(2)}, u32[]{:S(2)}) async-start(bf16[8,4,256,128]{3,2,1,0:T(8,128)(2,1)} %bitcast.13), calls=%async_computation.2 | async-start | bytes 4194304 | tf_op jit(solution)/shard_map/all_to_all | solution.py:237
  95.4 56.1 %copy-start.9 = (f32[256]{0:T(256)S(1)}, f32[256]{0:T(256)}, u32[]{:S(2)}) copy-start(f32[256]{0:T(256)} %constant.68) | copy-start | bytes 3076
  95.4 56.2 %copy-start.7 = (f32[64]{0:T(128)S(1)}, f32[64]{0:T(128)}, u32[]{:S(2)}) copy-start(f32[64]{0:T(128)} %defocus.3) | copy-start | bytes 772
  95.4 54.9 %collective-permute-start.3 = (bf16[25,128,128]{2,1,0:T(8,128)(2,1)}, bf16[25,128,128]{2,1,0:T(8,128)(2,1)S(1)}, u32[]{:S(2)}, u32[]{:S(2)}) collective-permute-start(bf16[25,128,128]{2,1,0:T(8,128)(2,1)} %get-tuple-element.27), channel_id=1, source_target_pairs={{0,1},{1,2},{2,3},{3,0},{4,5},{5,6},{6,7},{7,4},{8,9},{9,10},{10,1... | collective-permute-start | bytes 2457608 | tf_op jit(solution)/shard_map/ppermute | solution.py:310
  96.9 72.4 %collective-permute-start.4 = (bf16[25,128,128]{2,1,0:T(8,128)(2,1)}, bf16[25,128,128]{2,1,0:T(8,128)(2,1)S(1)}, u32[]{:S(2)}, u32[]{:S(2)}) collective-permute-start(bf16[25,128,128]{2,1,0:T(8,128)(2,1)} %get-tuple-element.28), channel_id=1, source_target_pairs={{0,2},{1,3},{2,0},{3,1},{4,6},{5,7},{6,4},{7,5},{8,10},{9,11},{10,... | collective-permute-start | bytes 2457608 | tf_op jit(solution)/shard_map/ppermute | solution.py:310
  98.4 70.9 %collective-permute-start.5 = (bf16[25,128,128]{2,1,0:T(8,128)(2,1)}, bf16[25,128,128]{2,1,0:T(8,128)(2,1)}, u32[]{:S(2)}, u32[]{:S(2)}) collective-permute-start(bf16[25,128,128]{2,1,0:T(8,128)(2,1)} %get-tuple-element.29), channel_id=1, source_target_pairs={{0,3},{1,0},{2,1},{3,2},{4,7},{5,4},{6,5},{7,6},{8,11},{9,8},{10,9... | collective-permute-start | bytes 2457608 | tf_op jit(solution)/shard_map/ppermute | solution.py:310
  135.8 49.8 %copy-start.4 = (bf16[256,512]{1,0:T(8,128)(2,1)S(1)}, bf16[256,512]{1,0:T(8,128)(2,1)}, u32[]{:S(2)}) copy-start(bf16[256,512]{1,0:T(8,128)(2,1)} %constant.59.clone.refs_9_) | copy-start | bytes 786436
  146.1 0.9 copy-start.2
  147.0 22.4 %collective-permute-start.6 = (bf16[25,128,128]{2,1,0:T(8,128)(2,1)}, bf16[25,128,128]{2,1,0:T(8,128)(2,1)}, u32[]{:S(2)}, u32[]{:S(2)}) collective-permute-start(bf16[25,128,128]{2,1,0:T(8,128)(2,1)} %get-tuple-element.32), channel_id=1, source_target_pairs={{0,1},{1,2},{2,3},{3,0},{4,5},{5,6},{6,7},{7,4},{8,9},{9,10},{10,1... | collective-permute-start | bytes 2457608 | tf_op jit(solution)/shard_map/ppermute | solution.py:310
  148.4 37.1 %collective-permute-start.7 = (bf16[25,128,128]{2,1,0:T(8,128)(2,1)}, bf16[25,128,128]{2,1,0:T(8,128)(2,1)}, u32[]{:S(2)}, u32[]{:S(2)}) collective-permute-start(bf16[25,128,128]{2,1,0:T(8,128)(2,1)} %get-tuple-element.33), channel_id=1, source_target_pairs={{0,2},{1,3},{2,0},{3,1},{4,6},{5,7},{6,4},{7,5},{8,10},{9,11},{10,... | collective-permute-start | bytes 2457608 | tf_op jit(solution)/shard_map/ppermute | solution.py:310
  150.3 35.3 %collective-permute-start.8 = (bf16[25,128,128]{2,1,0:T(8,128)(2,1)}, bf16[25,128,128]{2,1,0:T(8,128)(2,1)}, u32[]{:S(2)}, u32[]{:S(2)}) collective-permute-start(bf16[25,128,128]{2,1,0:T(8,128)(2,1)} %get-tuple-element.34), channel_id=1, source_target_pairs={{0,3},{1,0},{2,1},{3,2},{4,7},{5,4},{6,5},{7,6},{8,11},{9,8},{10,9... | collective-permute-start | bytes 2457608 | tf_op jit(solution)/shard_map/ppermute | solution.py:310
  151.5 34.1 %copy-start.3 = (bf16[25,128,128]{2,1,0:T(8,128)(2,1)S(1)}, bf16[25,128,128]{2,1,0:T(8,128)(2,1)}, u32[]{:S(2)}) copy-start(bf16[25,128,128]{2,1,0:T(8,128)(2,1)} %copy-done.2) | copy-start | bytes 2457604
  168.0 1.2 copy-start
